TPU v7x, 128 devices: a whole 4x4x4 slice. The times are simulated.
128 devices in a mesh: seq: 16 (over y, x_hi, core), head: 8 (over x_lo, z).
Axes of the slice: x: 4 (x_hi: 2, x_lo: 2; x = x_hi * 2 + x_lo), y: 4, z: 4, core: 2. Of those that a mesh axis runs over, the one named last changes fastest.
Arguments:
- hidden: bfloat16 [2048, 8192], P('head', 'seq'), may hold values from -6 to 6
- cross_query: bfloat16 [2048, 8192], P('seq', 'head'), may hold values from -128 to 128
- image_cache: bfloat16 [16, 1600, 2048], P('seq', None, 'head'), may hold values from -48 to 48
- features: bfloat16 [16, 1600, 8192], P('seq', None, 'head'), may hold values from -6 to 6
- image_proj: bfloat16 [8192, 2048], P('head'), may hold values from -0.5 to 0.5
- key_gain: float32 [128], replicated, may hold values from 0.1 to 1.9
- out_weight: bfloat16 [8192, 8192], P('head', 'seq'), may hold values from -0.0625 to 0.0625
- cross_gate: float32 [1], replicated, may hold values from 0.5 to 1.5
- image_spans: int32 [2048, 2], replicated, may hold values from 0 to 16, as said below
- evicted: int32 [2], replicated, may hold values from 0 to 15, as said below
- placement: int32 [16], replicated, may hold values from 0 to 15, as said below
Outputs:
- layer_output: bfloat16 [2048, 8192], P('head', 'seq')
Inputs may be any that keep to these rules, and one draw needn't show every extreme that they name: `image_spans`: row t holds the first image that token t sees and one past the last; the first is below the last, the last is at least 8, and the last never decreases as t grows. `evicted`: 2 distinct image ids. `placement`: each image id appears in exactly one slot.
All inputs are finite; a program needn't handle non-finite values.
Results may differ from a plain program's by a relative error of at most 0.038.
Values may be sent and summed in bfloat16 or wider, within the bound.
No kernel may reach another device: no remote copies, remote signals or barrier semaphores. Data moves between devices by JAX's collectives and lax.ppermute only.
A program may use at most 128 MiB of HBM per device.

v0:
```python
import jax
import jax.numpy as jnp
from jax import lax
from jax.sharding import PartitionSpec as P

MASKED_SCORE = -1e30


def in_blocks(x, dim, peers):
    dims = x.shape
    blocks = x.reshape(*dims[:dim], peers, dims[dim] // peers, *dims[dim + 1 :])
    return jnp.moveaxis(blocks, dim, 0)


def sum_at_owner(x, axis, dim):
    blocks = in_blocks(x, dim, lax.axis_size(axis))
    arrived = lax.all_to_all(blocks, axis, split_axis=0, concat_axis=0, tiled=True)
    return arrived.astype(jnp.float32).sum(axis=0)


def block_size(row_count):
    block_len = row_count
    while block_len > 1024 and block_len % 2 == 0:
        block_len = block_len // 2
    return block_len


def empty_state(row_count, groups, per_group, head_size):
    return (
        jnp.full((row_count, groups, per_group), MASKED_SCORE, jnp.float32),
        jnp.zeros((row_count, groups, per_group), jnp.float32),
        jnp.zeros((row_count, groups, per_group, head_size), jnp.float32),
    )


def absorb(carry_state, queries, key_values, allowed):
    highest, weight_sum, weighted = carry_state
    head_size = queries.shape[-1]
    scores = jnp.einsum(
        "rgqd,ngd->rgqn", queries, key_values[:, :, 0], preferred_element_type=jnp.float32
    ) * head_size ** (-0.5)
    visible = allowed[:, None, None, :]
    renewed = jnp.maximum(highest, jnp.max(jnp.where(visible, scores, MASKED_SCORE), axis=-1))
    weights = jnp.where(visible, jnp.exp(scores - renewed[..., None]), 0.0)
    rescale = jnp.exp(highest - renewed)
    weight_sum = weight_sum * rescale + jnp.sum(weights, axis=-1)
    weighted = weighted * rescale[..., None] + jnp.einsum(
        "rgqn,ngd->rgqd",
        weights.astype(jnp.bfloat16),
        key_values[:, :, 1],
        preferred_element_type=jnp.float32,
    )
    return (renewed, weight_sum, weighted)


def sweep_keys(carry_state, queries, key_values, key_labels, allow):
    row_count = key_values.shape[0]
    block_len = block_size(row_count)
    block_count = row_count // block_len
    blocks = key_values.reshape((block_count, block_len) + key_values.shape[1:])
    labels = key_labels.reshape(block_count, block_len)

    def advance(current, element):
        return (absorb(current, queries, element[0], allow(element[1])), None)

    carry_state, unused = lax.scan(advance, carry_state, (blocks, labels))
    return carry_state


def on_device(
    hidden,
    cross_query,
    image_cache,
    features,
    image_proj,
    key_gain,
    out_weight,
    cross_gate,
    image_spans,
    evicted,
    placement,
):
    head_size = key_gain.shape[0]
    groups = image_cache.shape[2] // (2 * head_size)
    per_group = cross_query.shape[1] // (groups * head_size)
    heads_here = groups * per_group
    local_cols = groups * 2 * head_size
    tok_rows = cross_query.shape[0]
    seq_pos = lax.axis_index("seq")
    patches = features.shape[1]
    own_image = lax.dynamic_index_in_dim(placement, seq_pos, 0, keepdims=False)
    evicted_here = jnp.any(evicted == own_image)
    cached = image_cache[0].reshape(patches, groups, 2, head_size)
    own_rows = features[0]
    partial_value = lax.cond(
        evicted_here,
        lambda: jnp.dot(own_rows, image_proj, preferred_element_type=jnp.float32),
        lambda: jnp.zeros((patches, image_proj.shape[1]), jnp.float32),
    )
    summed = lax.psum_scatter(
        partial_value.astype(jnp.bfloat16), "head", scatter_dimension=1, tiled=True
    ).astype(jnp.float32)
    grouped = summed.reshape(summed.shape[:-1] + (groups, 2, head_size))
    key_cols = grouped[..., 0, :]
    inverse = lax.rsqrt(jnp.mean(key_cols * key_cols, axis=-1, keepdims=True) + 1e-05)
    key_cols = key_cols * inverse * key_gain
    rebuilt = jnp.stack([key_cols, grouped[..., 1, :]], axis=-2).astype(jnp.bfloat16)
    slot_kv = jnp.where(evicted_here, rebuilt, cached)
    slot_ids = jnp.full((patches,), own_image, jnp.int32)
    first_image = image_spans[:, 0]
    stop_image = image_spans[:, 1]
    own_first = lax.dynamic_slice_in_dim(first_image, seq_pos * tok_rows, tok_rows)
    own_stop = lax.dynamic_slice_in_dim(stop_image, seq_pos * tok_rows, tok_rows)
    image_queries = cross_query.reshape(tok_rows, groups, per_group, head_size)

    def inside(key_labels):
        return (key_labels[None, :] >= own_first[:, None]) & (
            key_labels[None, :] < own_stop[:, None]
        )

    slot_flat = slot_kv.reshape(slot_kv.shape[0], local_cols)
    kv_portion = lax.all_gather(slot_flat[None], "seq", axis=0, tiled=True)
    id_portion = lax.all_gather(slot_ids[None], "seq", axis=0, tiled=True)
    image_state = sweep_keys(
        empty_state(tok_rows, groups, per_group, head_size),
        image_queries,
        kv_portion.reshape(-1, groups, 2, head_size),
        id_portion.reshape(-1),
        inside,
    )
    cross_context = (
        (image_state[2] / image_state[1][..., None])
        .reshape(tok_rows, heads_here * head_size)
        .astype(jnp.bfloat16)
    )
    partial_out = jnp.dot(
        lax.all_gather(cross_context, "seq", axis=0, tiled=True),
        out_weight,
        preferred_element_type=jnp.float32,
    )
    summed_out = sum_at_owner(partial_out.astype(jnp.bfloat16), "head", 0)
    layer_output = (hidden.astype(jnp.float32) + jnp.tanh(cross_gate[0]) * summed_out).astype(
        jnp.bfloat16
    )
    return layer_output


def solution(mesh):
    placed = (
        P("head", "seq"),
        P("seq", "head"),
        P("seq", None, "head"),
        P("seq", None, "head"),
        P("head", None),
        P(),
        P("head", "seq"),
        P(),
        P(),
        P(),
        P(),
    )
    return jax.shard_map(
        on_device, mesh=mesh, in_specs=placed, out_specs=P("head", "seq"), check_vma=False
    )
```

profile of v0, /device:TPU:0, one launch (start us, length us, event | category | flops | bytes accessed | tf_op | source)
XLA Modules:
  0.0 565.7 jit_solution(17945741866223766300)
XLA Ops:
  10.4 3.6 conditional.1
  10.4 3.6 broadcast.63
  15.8 83.7 %reduce-scatter.2.cloned.1.call-done = bf16[1600,256]{1,0:T(8,128)(2,1)} async-done(((bf16[1600,2048]{1,0:T(8,128)(2,1)}), bf16[1600,256]{1,0:T(8,128)(2,1)}) %reduce-scatter.2.cloned.1.call-update) | async-done | bytes 819216 | tf_op jit(solution)/shard_map/reduce_scatter | solution.py:100
  113.7 13.6 %all-reduce = s32[16]{0:T(128)S(1)} all-reduce(s32[16]{0:T(128)S(1)} %dynamic-update-slice), channel_id=3, replica_groups=mesh['seq'=16,'head'=8] {'seq'}, use_global_device_ids=true, to_apply=%add | all-reduce | flops 16 | bytes 128
  127.9 75.3 %all-gather.4.cloned.1.call-done = bf16[16,1600,256]{2,1,0:T(8,128)(2,1)} async-done(((bf16[1,1600,256]{2,1,0:T(8,128)(2,1)}), bf16[16,1600,256]{2,1,0:T(8,128)(2,1)}) %all-gather.4.cloned.1.call-update) | async-done | bytes 13107216 | tf_op jit(solution)/shard_map/all_gather | solution.py:122
  203.2 19.0 %reshape_reshape.7 = bf16[32,800,1,2,128]{4,3,1,0,2:T(2,128)(2,1)} reshape(bf16[16,1600,256]{2,1,0:T(8,128)(2,1)} %all-gather.4.cloned.1.call-done) | data formatting | bytes 26214400 | tf_op jit(solution)/shard_map/reshape;reshape | solution.py:60
  222.2 243.7 %while.15 = (s32[]{:T(128)}, f32[128,1,8]{0,2,1:T(8,128)S(1)}, f32[128,1,8]{0,2,1:T(8,128)S(1)}, f32[128,1,8,128]{0,3,2,1:T(8,128)S(1)}, s32[32,800]{1,0:T(8,128...) while((s32[]{:T(128)}, f32[128,1,8]{0,2,1:T(8,128)S(1)}, ...), condition=%wide.region_8.9_spmd.clone, body=%wide.region_5.8_spmd.clone.sunk | while | flops 429148160 | bytes 26782236 | solution.py:66
  223.7 2.3 fusion.36
  226.0 3.0 fusion.39
  233.6 3.0 fusion.39
  239.0 2.3 fusion.36
  241.3 3.0 fusion.39
  248.9 3.0 fusion.39
  254.2 2.3 fusion.36
  256.5 3.0 fusion.39
  264.1 3.0 fusion.39
  269.4 2.3 fusion.36
  271.7 3.0 fusion.39
  279.3 3.0 fusion.39
  287.0 3.0 fusion.39
  294.6 3.0 fusion.39
  299.9 2.3 fusion.36
  302.2 3.0 fusion.39
  309.8 3.0 fusion.39
  317.4 3.0 fusion.39
  325.0 3.0 fusion.39
  332.7 3.0 fusion.39
  340.3 3.0 fusion.39
  347.9 3.0 fusion.39
  355.5 3.0 fusion.39
  363.1 3.0 fusion.39
  370.7 3.0 fusion.39
  378.4 3.0 fusion.39
  386.0 3.0 fusion.39
  393.6 3.0 fusion.39
  401.2 3.0 fusion.39
  408.8 3.0 fusion.39
  416.4 3.0 fusion.39
  424.1 3.0 fusion.39
  431.7 3.0 fusion.39
  439.3 3.0 fusion.39
  446.9 3.0 fusion.39
  454.5 3.0 fusion.39
  462.1 3.0 fusion.39
  466.7 54.5 %all-gather.6.cloned.1.call-done = bf16[2048,1024]{0,1:T(8,128)(2,1)} async-done(((bf16[128,1024]{0,1:T(8,128)(2,1)}), bf16[2048,1024]{0,1:T(8,128)(2,1)}) %all-gather.6.cloned.1.call-update) | async-done | bytes 4194320 | tf_op jit(solution)/shard_map/all_gather | solution.py:137
  521.2 5.9 %convolution_convert_fusion = bf16[2048,512]{1,0:T(8,128)(2,1)} fusion(bf16[2048,1024]{0,1:T(8,128)(2,1)} %all-gather.6.cloned.1.call-done, bf16[1024,512]{1,0:T(8,128)(2,1)S(1)} %copy-done), kind=kOutput, calls=%fused_computation.31 | convolution fusion | flops 2148532224 | bytes 7340032 | tf_op jit(solution)/shard_map/dot_general | solution.py:136
  527.1 4.6 all-to-all-start
  532.3 25.8 %all-to-all-done = bf16[8,256,512]{2,1,0:T(8,128)(2,1)S(1)} async-done(((bf16[8,256,512]{2,1,0:T(8,128)(2,1)}), bf16[8,256,512]{2,1,0:T(8,128)(2,1)S(1)}, u32[]{:S(2)}, u32[]{:S(2)}) %all-to-all-start) | async-done | bytes 2097184 | tf_op jit(solution)/shard_map/all_to_all | solution.py:17
  (396 shorter events, 154.8 us)
Async XLA Ops:
  6.5 514.7 %copy-start = (bf16[1024,512]{1,0:T(8,128)(2,1)S(1)}, bf16[1024,512]{1,0:T(8,128)(2,1)}, u32[]{:S(2)}) copy-start(bf16[1024,512]{1,0:T(8,128)(2,1)} %param.21) | copy-start | bytes 3145732
  6.5 92.9 %reduce-scatter.2.cloned.1.call-start = ((), (), s32[]{:S(2)}) async-start(), calls=%async_computation.2 | async-start | bytes 7372800 | tf_op jit(solution)/shard_map/reduce_scatter | solution.py:100
  13.9 1.1 copy-start.2
  14.0 90.8 %copy-start.6 = (f32[128]{0:T(128)S(1)}, f32[128]{0:T(128)}, u32[]{:S(2)}) copy-start(f32[128]{0:T(128)} %param.20) | copy-start | bytes 1540
  14.0 189.2 %all-gather.4.cloned.1.call-start = ((), (), s32[]{:S(2)}) async-start(), calls=%async_computation.3 | async-start | bytes 13926400 | tf_op jit(solution)/shard_map/all_gather | solution.py:122
  106.0 5.6 copy-start.7
  106.0 21.4 %copy-start.3 = (bf16[128,1024]{1,0:T(8,128)(2,1)S(1)}, bf16[128,1024]{1,0:T(8,128)(2,1)}, u32[]{:S(2)}) copy-start(bf16[128,1024]{1,0:T(8,128)(2,1)} %param.16) | copy-start | bytes 786436
  107.6 20.2 %copy-start.5 = (s32[2048,2]{0,1:T(2,128)S(1)}, s32[2048,2]{0,1:T(2,128)}, u32[]{:S(2)}) copy-start(s32[2048,2]{0,1:T(2,128)} %param.23) | copy-start | bytes 49156
  111.5 409.7 %all-gather.6.cloned.1.call-start = ((), (), s32[]{:S(2)}) async-start(), calls=%async_computation.4 | async-start | bytes 4456448 | tf_op jit(solution)/shard_map/all_gather | solution.py:137
  226.0 3.0 copy-start.1
  233.6 3.0 copy-start.1
  241.2 3.0 copy-start.1
  248.9 3.0 copy-start.1
  256.5 3.0 copy-start.1
  264.1 3.0 copy-start.1
  271.7 3.0 copy-start.1
  279.3 3.0 copy-start.1
  286.9 3.0 copy-start.1
  294.6 3.0 copy-start.1
  302.2 3.0 copy-start.1
  309.8 3.0 copy-start.1
  317.4 3.0 copy-start.1
  325.0 3.0 copy-start.1
  332.6 3.0 copy-start.1
  340.3 3.0 copy-start.1
  347.9 3.0 copy-start.1
  355.5 3.0 copy-start.1
  363.1 3.0 copy-start.1
  370.7 3.0 copy-start.1
  378.3 3.0 copy-start.1
  386.0 3.0 copy-start.1
  393.6 3.0 copy-start.1
  401.2 3.0 copy-start.1
  408.8 3.0 copy-start.1
  416.4 3.0 copy-start.1
  424.0 3.0 copy-start.1
  431.7 3.0 copy-start.1
  439.3 3.0 copy-start.1
  446.9 3.0 copy-start.1
  454.5 3.0 copy-start.1
  462.1 3.0 copy-start.1
  527.1 31.3 %copy-start.4 = (bf16[256,512]{1,0:T(8,128)(2,1)S(1)}, bf16[256,512]{1,0:T(8,128)(2,1)}, u32[]{:S(2)}) copy-start(bf16[256,512]{1,0:T(8,128)(2,1)} %param.15) | copy-start | bytes 786436
  527.1 31.0 %all-to-all-start = ((bf16[8,256,512]{2,1,0:T(8,128)(2,1)}), bf16[8,256,512]{2,1,0:T(8,128)(2,1)S(1)}, u32[]{:S(2)}, u32[]{:S(2)}) async-start(bf16[8,256,512]{2,1,0:T(8,128)(2,1)} %bitcast.110), calls=%async_computation.1 | async-start | bytes 4194304 | tf_op jit(solution)/shard_map/all_to_all | solution.py:17
Sparse Core Ops, SparseCore 0:
  14.1 85.2 reduce-scatter.1
  111.6 91.5 all-gather.3
  466.8 54.3 all-gather.5
where the time goes:
time: 569 us; the launch traced here: 566 us
  waiting for transfers between devices  239 us (42%)
  matrix products  175 us (31%)
  local copies, waits for them, and re-layouts  80.8 us (14%)
  other arithmetic  34.9 us (6%)
  between operations  14.6 us (3%)
  blocking collectives  13.6 us (2%)
    dot_general x32, matrix products, absorb(): jnp.einsum('rgqn,ngd->rgqd', weights.astype(jnp.bfloat16), key_values[:,...  96.6 us
    reduce_scatter x1, waiting for transfers between devices, on_device(): lax.psum_scatter(partial_value.astype(jnp.bfloat16), 'head', scatter_dime...  83.7 us
    all_gather x1, waiting for transfers between devices, on_device(): kv_portion = lax.all_gather(slot_flat[None], 'seq', axis=0, tiled=True)  75.3 us
    dot_general x32, matrix products, absorb(): jnp.einsum('rgqd,ngd->rgqn', queries, key_values[:, :, 0], preferred_elem...  72.9 us
    all_gather x1, waiting for transfers between devices, on_device(): lax.all_gather(cross_context, 'seq', axis=0, tiled=True)  54.5 us
    dynamic_slice x96, local copies, waits for them, and re-layouts, sweep_keys(): carry_state, unused = lax.scan(advance, carry_state, (blocks, labels))  43.7 us
    all_to_all x1, waiting for transfers between devices, sum_at_owner(): lax.all_to_all(blocks, axis, split_axis=0, concat_axis=0, tiled=True)  25.8 us
    reduce_sum x32, other arithmetic, absorb(): weight_sum = weight_sum * rescale + jnp.sum(weights, axis=-1)  21.7 us
  transfers between devices with their start and end apart: 4, of which 4 were waited for; matrix products, arithmetic and copies ran while one was open for 1% of the time, Pallas kernels for 0%

commit v1 on v0

v1 whole, which is shorter than its diff:
```python
import functools
import math

import jax
import jax.numpy as jnp
from jax import lax
from jax.experimental import pallas as pl
from jax.experimental.pallas import tpu as pltpu
from jax.sharding import PartitionSpec as P

MASKED_SCORE = -1e30


def in_blocks(x, dim, peers):
    dims = x.shape
    blocks = x.reshape(*dims[:dim], peers, dims[dim] // peers, *dims[dim + 1 :])
    return jnp.moveaxis(blocks, dim, 0)


def sum_at_owner(x, axis, dim):
    blocks = in_blocks(x, dim, lax.axis_size(axis))
    arrived = lax.all_to_all(blocks, axis, split_axis=0, concat_axis=0, tiled=True)
    return arrived.astype(jnp.float32).sum(axis=0)


def attend_kernel(head_size, heads, ids_ref, q_ref, first_ref, stop_ref, kv_ref, out_ref, m_ref, l_ref, acc_ref):
    step = pl.program_id(0)
    tokens = q_ref.shape[0]
    factor = math.log2(math.e) * head_size ** (-0.5)

    @pl.when(step == 0)
    def _():
        m_ref[...] = jnp.full_like(m_ref, MASKED_SCORE)
        l_ref[...] = jnp.zeros_like(l_ref)
        acc_ref[...] = jnp.zeros_like(acc_ref)

    image = ids_ref[step]
    keys = kv_ref[0, :, :head_size]
    values = kv_ref[0, :, head_size:]
    seen = (first_ref[...] <= image) & (image < stop_ref[...])
    for pair in range(heads // 2):
        rows = pl.ds(pair * 2 * tokens, 2 * tokens)
        cols = pair * 2 * head_size
        queries = jnp.concatenate(
            [q_ref[:, cols : cols + head_size], q_ref[:, cols + head_size : cols + 2 * head_size]], axis=0
        )
        scores = lax.dot_general(queries, keys, (((1,), (1,)), ((), ())), preferred_element_type=jnp.float32)
        here = jnp.max(scores, axis=1, keepdims=True)
        weights = jnp.exp2((scores - here) * factor)
        total = jnp.sum(weights, axis=1, keepdims=True)
        mixed = jnp.dot(weights.astype(jnp.bfloat16), values, preferred_element_type=jnp.float32)
        before = m_ref[rows, :]
        after = jnp.where(seen, jnp.maximum(before, here), before)
        keep = jnp.exp2((before - after) * factor)
        add = jnp.where(seen, jnp.exp2((here - after) * factor), 0.0)
        m_ref[rows, :] = after
        l_ref[rows, :] = l_ref[rows, :] * keep + add * total
        acc_ref[rows, :] = acc_ref[rows, :] * keep + add * mixed

    @pl.when(step == pl.num_programs(0) - 1)
    def _():
        for head in range(heads):
            rows = pl.ds(head * tokens, tokens)
            out_ref[:, head * head_size : (head + 1) * head_size] = (acc_ref[rows, :] / l_ref[rows, :]).astype(
                out_ref.dtype
            )


def attend(queries, key_values, ids, first, stop, head_size):
    tokens, cols = queries.shape
    heads = cols // head_size
    slots, rows, kv_cols = key_values.shape
    pair = lambda x: jnp.concatenate([x, x])[:, None]
    whole = lambda shape: pl.BlockSpec(shape, lambda i, ids: (0,) * len(shape))
    return pl.pallas_call(
        functools.partial(attend_kernel, head_size, heads),
        grid_spec=pltpu.PrefetchScalarGridSpec(
            num_scalar_prefetch=1,
            grid=(slots,),
            in_specs=[
                whole((tokens, cols)),
                whole((2 * tokens, 1)),
                whole((2 * tokens, 1)),
                pl.BlockSpec((1, rows, kv_cols), lambda i, ids: (i, 0, 0)),
            ],
            out_specs=whole((tokens, cols)),
            scratch_shapes=[
                pltpu.VMEM((heads * tokens, 1), jnp.float32),
                pltpu.VMEM((heads * tokens, 1), jnp.float32),
                pltpu.VMEM((heads * tokens, head_size), jnp.float32),
            ],
        ),
        out_shape=jax.ShapeDtypeStruct((tokens, cols), jnp.bfloat16),
        compiler_params=pltpu.CompilerParams(vmem_limit_bytes=40 * 1024 * 1024),
        name="attend",
    )(ids, queries, pair(first), pair(stop), key_values)


def on_device(
    hidden,
    cross_query,
    image_cache,
    features,
    image_proj,
    key_gain,
    out_weight,
    cross_gate,
    image_spans,
    evicted,
    placement,
):
    head_size = key_gain.shape[0]
    tok_rows = cross_query.shape[0]
    seq_pos = lax.axis_index("seq")
    patches = features.shape[1]
    own_image = lax.dynamic_index_in_dim(placement, seq_pos, 0, keepdims=False)
    evicted_here = jnp.any(evicted == own_image)
    own_rows = features[0]
    partial_value = lax.cond(
        evicted_here,
        lambda: jnp.dot(own_rows, image_proj, preferred_element_type=jnp.float32).astype(jnp.bfloat16),
        lambda: jnp.zeros((patches, image_proj.shape[1]), jnp.bfloat16),
    )
    summed = lax.psum_scatter(partial_value, "head", scatter_dimension=1, tiled=True).astype(jnp.float32)
    key_cols = summed[:, :head_size]
    inverse = lax.rsqrt(jnp.mean(key_cols * key_cols, axis=-1, keepdims=True) + 1e-05)
    key_cols = key_cols * inverse * key_gain
    rebuilt = jnp.concatenate([key_cols, summed[:, head_size:]], axis=1).astype(jnp.bfloat16)
    slot_kv = jnp.where(evicted_here, rebuilt, image_cache[0])
    own_spans = lax.dynamic_slice_in_dim(image_spans, seq_pos * tok_rows, tok_rows)
    key_values = lax.all_gather(slot_kv, "seq", axis=0)
    cross_context = attend(cross_query, key_values, placement, own_spans[:, 0], own_spans[:, 1], head_size)
    partial_out = jnp.dot(
        lax.all_gather(cross_context, "seq", axis=0, tiled=True),
        out_weight,
        preferred_element_type=jnp.float32,
    )
    summed_out = sum_at_owner(partial_out.astype(jnp.bfloat16), "head", 0)
    layer_output = (hidden.astype(jnp.float32) + jnp.tanh(cross_gate[0]) * summed_out).astype(jnp.bfloat16)
    return layer_output


def solution(mesh):
    placed = (
        P("head", "seq"),
        P("seq", "head"),
        P("seq", None, "head"),
        P("seq", None, "head"),
        P("head", None),
        P(),
        P("head", "seq"),
        P(),
        P(),
        P(),
        P(),
    )
    return jax.shard_map(
        on_device, mesh=mesh, in_specs=placed, out_specs=P("head", "seq"), check_vma=False
    )
```

time: 569 us -> 353 us (0.62)
  matrix products: 175 us -> 5.86 us
  local copies, waits for them, and re-layouts: 80.8 us -> 11.6 us
  Pallas kernels: 0 us -> 52.4 us
  other arithmetic: 34.9 us -> 7.53 us
  waiting for transfers between devices: 239 us -> 254 us
  blocking collectives: 13.6 us -> 0 us
    dot_general x64 -> x0, matrix products: 169 us -> none  [the longest x32 96.6 us: absorb(): jnp.einsum('rgqn,ngd->rgqd', weights.astype(jnp.bfloat16), key_values[:,...]
    pallas_call x0 -> x1, Pallas kernels: none -> 52.4 us  [attend(): pl.pallas_call(functools.partial(attend_kernel, head_size, heads), grid_s...]
    dynamic_slice x97 -> x1, local copies, waits for them, and re-layouts: 43.8 us -> 0.68 us  [on_device(): lax.dynamic_slice_in_dim(image_spans, seq_pos * tok_rows, tok_rows)]
    reduce_sum x32 -> x0, other arithmetic: 21.7 us -> none  [absorb(): weight_sum = weight_sum * rescale + jnp.sum(weights, axis=-1)]
    another operation x4 -> x1, local copies, waits for them, and re-layouts: 24.2 us -> 3.56 us  [the longest x1 19 us: sweep_keys(): blocks = key_values.reshape((block_count, block_len) + key_values.shape[1:])]
    all_gather x1, waiting for transfers between devices: 75.3 us -> 90.6 us  [on_device(): key_values = lax.all_gather(slot_kv, 'seq', axis=0)]
    unnamed x1 -> x0, blocking collectives: 13.6 us -> none
  transfers between devices with their start and end apart: 4 -> 4, of which waited for: 4 -> 4; matrix products, arithmetic and copies ran while one was open for 1% -> 0% of each run, Pallas kernels for 0% -> 0%
where the time goes in v1:
time: 353 us; the launch traced here: 351 us
  waiting for transfers between devices  254 us (72%)
  Pallas kernels  52.4 us (15%)
  between operations  14.6 us (4%)
  local copies, waits for them, and re-layouts  11.6 us (3%)
  other arithmetic  7.53 us (2%)
  matrix products  5.86 us (2%)
  starting transfers between devices  4.66 us (1%)
    all_gather x1, waiting for transfers between devices, on_device(): key_values = lax.all_gather(slot_kv, 'seq', axis=0)  90.6 us
    reduce_scatter x1, waiting for transfers between devices, on_device(): lax.psum_scatter(partial_value, 'head', scatter_dimension=1, tiled=True)  84.5 us
    all_gather x1, waiting for transfers between devices, on_device(): lax.all_gather(cross_context, 'seq', axis=0, tiled=True)  53.1 us
    pallas_call x1, Pallas kernels, attend(): pl.pallas_call(functools.partial(attend_kernel, head_size, heads), grid_s...  52.4 us
    all_to_all x1, waiting for transfers between devices, sum_at_owner(): lax.all_to_all(blocks, axis, split_axis=0, concat_axis=0, tiled=True)  25.8 us
  transfers between devices with their start and end apart: 4, of which 4 were waited for; matrix products, arithmetic and copies ran while one was open for 0% of the time, Pallas kernels for 0%

profile of v1, /device:TPU:0, one launch (start us, length us, event | category | flops | bytes accessed | tf_op | source)
XLA Modules:
  0.0 350.7 jit_solution(17252164681695839260)
XLA Ops:
  6.5 0.0 copy-start
  6.5 0.0 reduce-scatter.2.cloned.1.call-start
  6.5 1.3 dynamic_slice.8
  7.9 2.0 compare_reduce_fusion
  10.5 3.6 %conditional.1 = (bf16[1600,2048]{1,0:T(8,128)(2,1)}) conditional(s32[]{:T(128)} %convert_element_type.28, () %tuple.11, (bf16[1,1600,1024]{2,1,0:T(8,128)(2,1)}, bf16[1024,2048]{1,0:T(8,128)(2,1)}) %tuple.12), branch_computations={%region_1.2_spmd, %region_2.3_spmd} | conditional | flops 6714163200 | bytes 14024712 | solution.py:119
  10.6 3.6 %broadcast.15 = bf16[1600,2048]{1,0:T(8,128)(2,1)} broadcast(bf16[]{:T(256)} %constant.8.clone), dimensions={} | broadcast | bytes 6553602 | tf_op jit(solution)/shard_map/broadcast.1
  14.1 0.0 copy-start.6
  14.1 0.0 copy-start.4
  14.1 0.0 reduce-scatter.2.cloned.1.call-update
  14.1 0.0 copy-start.2
  14.2 0.0 copy-start.3
  14.2 0.0 all-gather.3.cloned.1.call-start
  14.2 84.5 %reduce-scatter.2.cloned.1.call-done = bf16[1600,256]{1,0:T(8,128)(2,1)} async-done(((bf16[1600,2048]{1,0:T(8,128)(2,1)}), bf16[1600,256]{1,0:T(8,128)(2,1)}) %reduce-scatter.2.cloned.1.call-update) | async-done | bytes 819216 | tf_op jit(solution)/shard_map/reduce_scatter | solution.py:124
  98.7 1.3 fusion.1
  100.0 1.0 slice_bitcast_fusion
  101.0 0.0 copy-done.6
  101.1 1.3 fusion.4
  102.3 0.0 copy-done.4
  102.4 1.8 maximum_select_fusion
  104.2 0.0 all-gather.3.cloned.1.call-update
  104.2 0.0 all-gather.5.cloned.1.call-start
  104.3 0.7 constant_dynamic-slice_fusion
  105.0 0.1 copy.16.first_ref
  105.1 0.1 copy.17.stop_ref
  105.3 90.6 %all-gather.3.cloned.1.call-done.kv_ref = bf16[16,1600,256]{2,1,0:T(8,128)(2,1)} async-done(((bf16[1,1600,256]{2,1,0:T(8,128)(2,1)}), bf16[16,1600,256]{2,1,0:T(8,128)(2,1)}) %all-gather.3.cloned.1.call-update) | async-done | bytes 13107216 | tf_op jit(solution)/shard_map/all_gather | solution.py:131
  195.9 0.0 copy-done.2
  195.9 0.0 copy-done.3
  195.9 0.0 copy-start.1
  195.9 4.7 %copy-done.1 = bf16[16,1600,256]{2,1,0:T(8,128)(2,1)S(1)} copy-done((bf16[16,1600,256]{2,1,0:T(8,128)(2,1)S(1)}, bf16[16,1600,256]{2,1,0:T(8,128)(2,1)}, u32[]{:S(2)}) %copy-start.1) | copy-done | bytes 13107224
  200.6 52.4 %attend.1 = bf16[128,1024]{1,0:T(8,128)(2,1)} custom-call(s32[16]{0:T(128)S(1)} %copy-done.3, bf16[128,1024]{1,0:T(8,128)(2,1)S(1)} %copy-done.2, s32[256,1]{1,0:T(8,128)S(1)} %copy.16.first_ref, s32[256,1]{1,0:T(8,128)S(1)} %copy.17.stop_ref, bf16[16,1600,256]{2,1,0:T(8,128)(2,1)S(1)} %copy-done.1), custom_call_target="tpu_custom_call" | custom-call | tf_op jit(solution)/shard_map/attend/pallas_call | solution.py:75
  253.0 0.0 all-gather.5.cloned.1.call-update
  253.0 53.1 %all-gather.5.cloned.1.call-done = bf16[2048,1024]{1,0:T(8,128)(2,1)} async-done(((bf16[128,1024]{1,0:T(8,128)(2,1)}), bf16[2048,1024]{1,0:T(8,128)(2,1)}) %all-gather.5.cloned.1.call-update) | async-done | bytes 4194320 | tf_op jit(solution)/shard_map/all_gather | solution.py:134
  306.1 0.0 copy-done
  306.1 5.9 %convolution_convert_fusion.1 = bf16[2048,512]{1,0:T(8,128)(2,1)} fusion(bf16[2048,1024]{1,0:T(8,128)(2,1)} %all-gather.5.cloned.1.call-done, bf16[1024,512]{1,0:T(8,128)(2,1)S(1)} %copy-done), kind=kOutput, calls=%fused_computation.3 | convolution fusion | flops 2148532224 | bytes 7340032 | tf_op jit(solution)/shard_map/dot_general | solution.py:133
  312.0 0.0 copy-start.5
  312.0 4.6 %all-to-all-start = ((bf16[8,256,512]{2,1,0:T(8,128)(2,1)}), bf16[8,256,512]{2,1,0:T(8,128)(2,1)S(1)}, u32[]{:S(2)}, u32[]{:S(2)}) async-start(bf16[8,256,512]{2,1,0:T(8,128)(2,1)} %bitcast.19), calls=%async_computation.1 | async-start | bytes 4194304 | tf_op jit(solution)/shard_map/all_to_all | solution.py:22
  317.3 25.8 %all-to-all-done = bf16[8,256,512]{2,1,0:T(8,128)(2,1)S(1)} async-done(((bf16[8,256,512]{2,1,0:T(8,128)(2,1)}), bf16[8,256,512]{2,1,0:T(8,128)(2,1)S(1)}, u32[]{:S(2)}, u32[]{:S(2)}) %all-to-all-start) | async-done | bytes 2097184 | tf_op jit(solution)/shard_map/all_to_all | solution.py:22
  343.0 0.3 convert_reduce_fusion
  343.3 0.0 copy-done.5
  343.3 0.8 add_convert_fusion
  (3 shorter events, 0.0 us)
Async XLA Ops:
  6.5 299.6 %copy-start = (bf16[1024,512]{1,0:T(8,128)(2,1)S(1)}, bf16[1024,512]{1,0:T(8,128)(2,1)}, u32[]{:S(2)}) copy-start(bf16[1024,512]{1,0:T(8,128)(2,1)} %param.19) | copy-start | bytes 3145732
  6.5 92.1 %reduce-scatter.2.cloned.1.call-start = ((), (), s32[]{:S(2)}) async-start(), calls=%async_computation.2 | async-start | bytes 7372800 | tf_op jit(solution)/shard_map/reduce_scatter | solution.py:124
  14.1 86.9 %copy-start.6 = (f32[128]{0:T(128)S(1)}, f32[128]{0:T(128)}, u32[]{:S(2)}) copy-start(f32[128]{0:T(128)} %param.18) | copy-start | bytes 1540
  14.1 88.2 %copy-start.4 = (bf16[1,1600,256]{2,1,0:T(8,128)(2,1)S(1)}, bf16[1,1600,256]{2,1,0:T(8,128)(2,1)}, u32[]{:S(2)}) copy-start(bf16[1,1600,256]{2,1,0:T(8,128)(2,1)} %param.15) | copy-start | bytes 2457604
  14.1 181.7 %copy-start.2 = (bf16[128,1024]{1,0:T(8,128)(2,1)S(1)}, bf16[128,1024]{1,0:T(8,128)(2,1)}, u32[]{:S(2)}) copy-start(bf16[128,1024]{1,0:T(8,128)(2,1)} %q_ref.1) | copy-start | bytes 786436
  14.2 181.7 %copy-start.3 = (s32[16]{0:T(128)S(1)}, s32[16]{0:T(128)}, u32[]{:S(2)}) copy-start(s32[16]{0:T(128)} %ids_ref.1) | copy-start | bytes 196
  14.2 181.7 %all-gather.3.cloned.1.call-start = ((), (), s32[]{:S(2)}) async-start(), calls=%async_computation.3 | async-start | bytes 13926400 | tf_op jit(solution)/shard_map/all_gather | solution.py:131
  104.2 201.9 %all-gather.5.cloned.1.call-start = ((), (), s32[]{:S(2)}) async-start(), calls=%async_computation.4 | async-start | bytes 4456448 | tf_op jit(solution)/shard_map/all_gather | solution.py:134
  195.9 4.7 %copy-start.1 = (bf16[16,1600,256]{2,1,0:T(8,128)(2,1)S(1)}, bf16[16,1600,256]{2,1,0:T(8,128)(2,1)}, u32[]{:S(2)}) copy-start(bf16[16,1600,256]{2,1,0:T(8,128)(2,1)} %all-gather.3.cloned.1.call-done.kv_ref) | copy-start | bytes 39321604
  312.0 31.3 %copy-start.5 = (bf16[256,512]{1,0:T(8,128)(2,1)S(1)}, bf16[256,512]{1,0:T(8,128)(2,1)}, u32[]{:S(2)}) copy-start(bf16[256,512]{1,0:T(8,128)(2,1)} %param.13) | copy-start | bytes 786436
  312.0 31.0 %all-to-all-start = ((bf16[8,256,512]{2,1,0:T(8,128)(2,1)}), bf16[8,256,512]{2,1,0:T(8,128)(2,1)S(1)}, u32[]{:S(2)}, u32[]{:S(2)}) async-start(bf16[8,256,512]{2,1,0:T(8,128)(2,1)} %bitcast.19), calls=%async_computation.1 | async-start | bytes 4194304 | tf_op jit(solution)/shard_map/all_to_all | solution.py:22
Sparse Core Ops, SparseCore 0:
  14.3 84.3 reduce-scatter.1
  104.3 91.5 all-gather.2
  253.2 52.9 all-gather.4

commit v2 on v1

v2 whole, which is shorter than its diff:
```python
import functools
import math

import jax
import jax.numpy as jnp
from jax import lax
from jax.experimental import pallas as pl
from jax.experimental.pallas import tpu as pltpu
from jax.sharding import PartitionSpec as P

MASKED_SCORE = -1e30
CHUNK = 32
LIST = 18
VMEM = pltpu.CompilerParams(vmem_limit_bytes=48 * 1024 * 1024)


def seq_at(y, x, core):
    return (y % 4) * 4 + (x % 2) * 2 + core % 2


def head_at(x, z):
    return (x % 2) * 4 + z % 4


def send_seq(array, y=0, x=0, core=0):
    pairs = [
        (seq_at(a, b, c), seq_at(a + y, b + x, c + core)) for a in range(4) for b in range(2) for c in range(2)
    ]
    return lax.ppermute(array, "seq", pairs)


def send_head(array, x=0, z=0):
    return lax.ppermute(array, "head", [(head_at(a, b), head_at(a + x, b + z)) for a in range(2) for b in range(4)])


def add(*terms):
    return sum(term.astype(jnp.float32) for term in terms).astype(jnp.bfloat16)


def sum_over_head(parts):
    p00, p01, p10, p11, p20, p21, p30, p31 = parts
    via_x = send_head(p21, x=1)
    down = send_head(p31, z=-1)
    across = send_head(p11, x=1)
    p20 = add(p20, via_x)
    last = send_head(p30, z=-1)
    up = send_head(p20, z=1)
    p01 = add(p01, down)
    p10 = add(p10, across, up)
    side = send_head(p01, x=1)
    ahead = send_head(p10, z=1)
    return sum(term.astype(jnp.float32) for term in (p00, last, side, ahead))


def gather_chips(block):
    r30 = send_seq(block, y=1)
    r01 = send_seq(block, x=1)
    r10 = send_seq(block, y=-1)
    r20 = send_seq(r30, y=1)
    r31 = send_seq(r30, x=1)
    r11 = send_seq(r01, y=-1)
    r21 = send_seq(r20, x=1)
    return block, r01, r10, r11, r20, r21, r30, r31


def rebuild_kernel(order_ref, rows_ref, proj_ref, *out_refs):
    product = jnp.dot(rows_ref[...], proj_ref[...], preferred_element_type=jnp.float32).astype(jnp.bfloat16)
    for at, out_ref in enumerate(out_refs):

        @pl.when(pl.program_id(0) == at)
        def _():
            out_ref[...] = product


def rebuild_parts(rows, proj, order):
    count, depth = rows.shape
    cols = proj.shape[1] // 8
    return pl.pallas_call(
        rebuild_kernel,
        grid_spec=pltpu.PrefetchScalarGridSpec(
            num_scalar_prefetch=1,
            grid=(8,),
            in_specs=[
                pl.BlockSpec((count, depth), lambda i, order: (0, 0)),
                pl.BlockSpec((depth, cols), lambda i, order: (0, order[i])),
            ],
            out_specs=[pl.BlockSpec((count, cols), lambda i, order: (0, 0))] * 8,
        ),
        out_shape=[jax.ShapeDtypeStruct((count, cols), jnp.bfloat16)] * 8,
        compiler_params=VMEM,
        name="rebuild_parts",
    )(order, rows, proj)


def project_kernel(order_ref, core_ref, own_ref, other_ref, weight_ref, *out_refs):
    tokens = own_ref.shape[1]
    core = core_ref[0]
    own = jnp.dot(own_ref[0], weight_ref[...], preferred_element_type=jnp.float32).astype(jnp.bfloat16)
    other = jnp.dot(other_ref[0], weight_ref[...], preferred_element_type=jnp.float32).astype(jnp.bfloat16)
    for at, out_ref in enumerate(out_refs):

        @pl.when(pl.program_id(0) == at)
        def _():
            out_ref[pl.ds(pl.multiple_of(core * tokens, tokens), tokens), :] = own
            out_ref[pl.ds(pl.multiple_of((1 - core) * tokens, tokens), tokens), :] = other


def project_parts(own, other, weight, order, core):
    _, tokens, depth = own.shape
    cols = weight.shape[1]
    block = pl.BlockSpec((1, tokens, depth), lambda i, order, core: (order[i], 0, 0))
    return pl.pallas_call(
        project_kernel,
        grid_spec=pltpu.PrefetchScalarGridSpec(
            num_scalar_prefetch=2,
            grid=(8,),
            in_specs=[block, block, pl.BlockSpec((depth, cols), lambda i, order, core: (0, 0))],
            out_specs=[pl.BlockSpec((2 * tokens, cols), lambda i, order, core: (0, 0))] * 8,
        ),
        out_shape=[jax.ShapeDtypeStruct((2 * tokens, cols), jnp.bfloat16)] * 8,
        compiler_params=VMEM,
        name="project_parts",
    )(order, core, own, other, weight)


def sweep(head_size, ids_ref, count_ref, list_ref, q_ref, first_ref, stop_ref, kv_parts, m_ref, l_ref, acc_ref, even, odd):
    factor = math.log2(math.e) * head_size ** (-0.5)
    heads = q_ref.shape[1] // CHUNK

    for slot, (keys_of, values_of) in enumerate(kv_parts):
        count = count_ref[slot]

        def score(place, into):
            into[...] = lax.dot_general(
                q_ref[list_ref[slot * LIST + place]],
                keys_of(),
                (((1,), (1,)), ((), ())),
                preferred_element_type=jnp.float32,
            )

        def take(place, scores_ref):
            chunk = list_ref[slot * LIST + place]
            image = jnp.where(place < count, ids_ref[slot], -1)
            scores = scores_ref[...]
            here = jnp.max(scores, axis=1, keepdims=True)
            weights = jnp.exp2((scores - here) * factor)
            total = jnp.sum(weights, axis=1, keepdims=True)
            mixed = jnp.dot(weights.astype(jnp.bfloat16), values_of(), preferred_element_type=jnp.float32)
            tokens = pl.ds(pl.multiple_of(chunk * CHUNK, CHUNK), CHUNK)
            seen = (first_ref[tokens, :] <= image) & (image < stop_ref[tokens, :])
            seen = jnp.concatenate([seen.astype(jnp.int32)] * heads, axis=0) > 0
            before = m_ref[chunk]
            after = jnp.where(seen, jnp.maximum(before, here), before)
            keep = jnp.exp2((before - after) * factor)
            gain = jnp.where(seen, jnp.exp2((here - after) * factor), 0.0)
            m_ref[chunk] = after
            l_ref[chunk] = l_ref[chunk] * keep + gain * total
            acc_ref[chunk] = acc_ref[chunk] * keep + gain * mixed

        @pl.when(count > 0)
        def _():
            score(0, even)

            def body(at, carry):
                place = 2 * at
                score(place + 1, odd)
                take(place, even)
                score(place + 2, even)
                take(place + 1, odd)
                return carry

            lax.fori_loop(0, (count + 1) // 2, body, 0)


def held_kernel(head_size, ids, count, lists, q0, q1, q2, q3, order, first, stop, a, b, c, d, qs, m, l, acc, even, odd):
    heads = q0.shape[1] // head_size
    per_block = q0.shape[0] // CHUNK
    for block, q_ref in enumerate((q0, q1, q2, q3)):
        ordered = jnp.dot(order[block], q_ref[...], preferred_element_type=jnp.float32).astype(jnp.bfloat16)
        for part in range(per_block):
            for head in range(heads):
                qs[block * per_block + part, head * CHUNK : (head + 1) * CHUNK, :] = ordered[
                    part * CHUNK : (part + 1) * CHUNK, head * head_size : (head + 1) * head_size
                ]
    m[...] = jnp.full_like(m, MASKED_SCORE)
    l[...] = jnp.zeros_like(l)
    acc[...] = jnp.zeros_like(acc)
    kv_parts = [(lambda r=r: r[:, :head_size], lambda r=r: r[:, head_size:]) for r in (a, b, c, d)]
    sweep(head_size, ids, count, lists, qs, first, stop, kv_parts, m, l, acc, even, odd)


def rebuilt_kernel(
    head_size, ids, count, lists, qs, order, first, stop, m_in, l_in, acc_in, a, b, c, d, o0, o1, o2, o3, m, l, acc, even, odd
):
    factor = math.log2(math.e) * head_size ** (-0.5)
    tokens = o0.shape[0]
    heads = qs.shape[1] // CHUNK
    per_block = tokens // CHUNK
    m[...] = m_in[...]
    l[...] = l_in[...]
    acc[...] = acc_in[...]
    kv_parts = [
        (lambda r=r, i=i: r[i, :, :head_size], lambda r=r, i=i: r[i, :, head_size:])
        for r in (a, b, c, d)
        for i in range(2)
    ]
    sweep(head_size, ids, count, lists, qs, first, stop, kv_parts, m, l, acc, even, odd)
    lanes = lax.broadcasted_iota(jnp.int32, (tokens, 128), 1)
    for block, out in enumerate((o0, o1, o2, o3)):
        extra = jnp.zeros((tokens, 128), jnp.float32)
        for head in range(heads):
            rows = slice(head * CHUNK, (head + 1) * CHUNK)
            chunks = range(block * per_block, (block + 1) * per_block)
            high = jnp.concatenate([m[chunk, rows, :] for chunk in chunks], axis=0)
            total = jnp.concatenate([l[chunk, rows, :] for chunk in chunks], axis=0)
            mixed = jnp.concatenate([acc[chunk, rows, :] for chunk in chunks], axis=0)
            some = total > 0.0
            safe = jnp.where(some, total, 1.0)
            level = jnp.where(some, high * factor + jnp.log2(safe), MASKED_SCORE)
            ordered = (mixed / safe).astype(jnp.bfloat16)
            out[:, head * head_size : (head + 1) * head_size] = lax.dot_general(
                order[block], ordered, (((0,), (0,)), ((), ())), preferred_element_type=jnp.float32
            ).astype(jnp.bfloat16)
            for piece in range(3):
                rounded = level.astype(jnp.bfloat16).astype(jnp.float32)
                extra = jnp.where(lanes == piece * heads + head, rounded, extra)
                level = level - rounded
        out[:, heads * head_size :] = lax.dot_general(
            order[block], extra.astype(jnp.bfloat16), (((0,), (0,)), ((), ())), preferred_element_type=jnp.float32
        ).astype(jnp.bfloat16)


def merge_kernel(head_size, a, b, c, d, out):
    heads = out.shape[1] // head_size
    parts = (a, b, c, d)
    extras = [part[:, heads * head_size :].astype(jnp.float32) for part in parts]
    for head in range(heads):
        cols = slice(head * head_size, (head + 1) * head_size)
        levels = [sum(e[:, p * heads + head : p * heads + head + 1] for p in range(3)) for e in extras]
        top = functools.reduce(jnp.maximum, levels)
        shares = [jnp.exp2(level - top) for level in levels]
        mixed = sum(share * part[:, cols].astype(jnp.float32) for share, part in zip(shares, parts))
        out[:, cols] = (mixed / sum(shares)).astype(jnp.bfloat16)


def normalize(summed, key_gain):
    head_size = key_gain.shape[0]
    key_cols = summed[:, :head_size]
    inverse = lax.rsqrt(jnp.mean(key_cols * key_cols, axis=-1, keepdims=True) + 1e-05)
    return jnp.concatenate([key_cols * inverse * key_gain, summed[:, head_size:]], axis=1).astype(jnp.bfloat16)


def on_device(
    hidden,
    cross_query,
    image_cache,
    features,
    image_proj,
    key_gain,
    out_weight,
    cross_gate,
    image_spans,
    evicted,
    placement,
):
    head_size = key_gain.shape[0]
    tokens, cols = cross_query.shape
    heads = cols // head_size
    patches = features.shape[1]
    half = patches // 2
    seq_pos = lax.axis_index("seq")
    head_pos = lax.axis_index("head")
    y, x, core = seq_pos // 4, (seq_pos // 2) % 2, seq_pos % 2
    head_x, head_z = head_pos // 4, head_pos % 4
    chunks = 4 * tokens // CHUNK
    rows = heads * CHUNK

    own_part = lax.dynamic_slice_in_dim(features[0], core * half, half)
    sent_part = lax.dynamic_slice_in_dim(features[0], (1 - core) * half, half)
    peer_part = send_seq(sent_part, core=1)
    slots = placement.reshape(8, 2)
    stale = jnp.any(slots[:, :, None] == evicted, axis=-1)
    both = stale[:, 0] & stale[:, 1]
    chip = seq_pos // 2
    first_stale = stale[chip, 0]
    use_own = first_stale == (core == 0)
    home = jnp.stack([head_at(head_x + r % 2, head_z + r // 2) for r in range(8)]).astype(jnp.int32)

    def rebuild(part_rows):
        summed = sum_over_head(rebuild_parts(part_rows, image_proj, home))
        mine = normalize(summed, key_gain)
        pair = jnp.stack([mine, send_seq(mine, x=1)])
        return pair, send_seq(pair, core=1)

    held = image_cache[0]
    q_blocks = [cross_query] + [send_seq(cross_query, y=-dy) for dy in (1, 2, 3)]
    held_x = send_seq(held, x=1)
    held_core = send_seq(held, core=1)
    held_both = send_seq(held_x, core=1)

    spans = image_spans.reshape(16, tokens, 2)
    mine = jnp.stack(
        [lax.dynamic_index_in_dim(spans, seq_at(y + dy, x, core), 0, keepdims=False) for dy in range(4)]
    )
    first, stop = mine[:, :, 0], mine[:, :, 1]
    index = jnp.arange(tokens, dtype=jnp.int32)
    earlier = (first[:, None, :] < first[:, :, None]) | (
        (first[:, None, :] == first[:, :, None]) & (index[None, :] < index[:, None])[None]
    )
    rank = jnp.sum(earlier.astype(jnp.int32), axis=2)
    order = rank[:, None, :] == index[None, :, None]
    first = jnp.sum(jnp.where(order, first[:, None, :], 0), axis=2)
    stop = jnp.sum(jnp.where(order, stop[:, None, :], 0), axis=2)
    order = order.astype(jnp.bfloat16)
    chips = (chip, seq_at(y, x + 1, 0) // 2)
    held_ids = [slots[chips[0], core], slots[chips[0], 1 - core], slots[chips[1], core], slots[chips[1], 1 - core]]
    held_live = [
        ~stale[chips[0], core],
        ~stale[chips[0], 1 - core],
        ~stale[chips[1], core],
        ~stale[chips[1], 1 - core],
    ]
    once_ids = [jnp.where(stale[at, 0], slots[at, 0], slots[at, 1]) for at in chips]
    once_live = [stale[at, 0] | stale[at, 1] for at in chips]
    twice_ids = [slots[at, 1] for at in chips]
    twice_live = [both[at] for at in chips]
    ids = jnp.stack(held_ids + once_ids * 2 + twice_ids * 2).astype(jnp.int32)
    live = jnp.stack(held_live + once_live * 2 + twice_live * 2)
    seen = (first.reshape(1, chunks, CHUNK) <= ids[:, None, None]) & (
        ids[:, None, None] < stop.reshape(1, chunks, CHUNK)
    )
    wanted = jnp.any(seen, axis=2) & live[:, None]
    chunk_index = jnp.arange(chunks, dtype=jnp.int32)
    place = jnp.sum((wanted[:, None, :] & (chunk_index[None, :] < chunk_index[:, None])[None]).astype(jnp.int32), axis=2)
    lists = jnp.sum(
        jnp.where(
            wanted[:, None, :] & (place[:, None, :] == jnp.arange(LIST, dtype=jnp.int32)[None, :, None]),
            chunk_index[None, None, :],
            0,
        ),
        axis=2,
    )
    counts = jnp.sum(wanted.astype(jnp.int32), axis=1)
    first_col = first.reshape(4 * tokens, 1)
    stop_col = stop.reshape(4 * tokens, 1)

    state_shapes = [
        jax.ShapeDtypeStruct((chunks, rows, 1), jnp.float32),
        jax.ShapeDtypeStruct((chunks, rows, 1), jnp.float32),
        jax.ShapeDtypeStruct((chunks, rows, head_size), jnp.float32),
    ]
    smem = pl.BlockSpec(memory_space=pltpu.SMEM)
    vmem = pl.BlockSpec(memory_space=pltpu.VMEM)
    qs, high, total, mixed = pl.pallas_call(
        functools.partial(held_kernel, head_size),
        in_specs=[smem] * 3 + [vmem] * 11,
        out_specs=[vmem] * 4,
        out_shape=[jax.ShapeDtypeStruct((chunks, rows, head_size), jnp.bfloat16)] + state_shapes,
        scratch_shapes=[pltpu.VMEM((rows, patches), jnp.float32)] * 2,
        compiler_params=VMEM,
        name="attend_held",
    )(
        ids[:4], counts[:4], lists[:4].reshape(-1), *q_blocks, order, first_col, stop_col, held, held_core, held_x, held_both
    )

    once, once_core = rebuild(jnp.where(use_own, own_part, peer_part))
    nothing = jnp.zeros((2, half, 2 * head_size), jnp.bfloat16)
    twice, twice_core = lax.cond(
        jnp.any(both),
        lambda: rebuild(jnp.where(use_own, peer_part, own_part)),
        lambda: (nothing, nothing),
    )
    partial_out = pl.pallas_call(
        functools.partial(rebuilt_kernel, head_size),
        in_specs=[smem] * 3 + [vmem] * 11,
        out_specs=[vmem] * 4,
        out_shape=[jax.ShapeDtypeStruct((tokens, cols + 128), jnp.bfloat16)] * 4,
        scratch_shapes=[pltpu.VMEM(s.shape, s.dtype) for s in state_shapes]
        + [pltpu.VMEM((rows, half), jnp.float32)] * 2,
        compiler_params=VMEM,
        name="attend_rebuilt",
    )(
        ids[4:], counts[4:], lists[4:].reshape(-1), qs, order, first_col, stop_col, high, total, mixed,
        once, once_core, twice, twice_core,
    )
    arrived = [partial_out[0]] + [send_seq(partial_out[dy], y=dy) for dy in (1, 2, 3)]
    context = pl.pallas_call(
        functools.partial(merge_kernel, head_size),
        in_specs=[vmem] * 4,
        out_specs=vmem,
        out_shape=jax.ShapeDtypeStruct((tokens, cols), jnp.bfloat16),
        compiler_params=VMEM,
        name="merge",
    )(*arrived)

    own_context = jnp.stack(gather_chips(context))
    other_context = send_seq(own_context, core=1)
    source = []
    for r in range(8):
        target = head_at(head_x + r % 2, head_z + r // 2)
        source.append(2 * ((target // 2 - y) % 4) + (target % 2 - x) % 2)
    parts = project_parts(
        own_context, other_context, out_weight, jnp.stack(source).astype(jnp.int32), core.reshape(1).astype(jnp.int32)
    )
    summed_out = sum_over_head(parts)
    return (hidden.astype(jnp.float32) + jnp.tanh(cross_gate[0]) * summed_out).astype(jnp.bfloat16)


def solution(mesh):
    placed = (
        P("head", "seq"),
        P("seq", "head"),
        P("seq", None, "head"),
        P("seq", None, "head"),
        P("head", None),
        P(),
        P("head", "seq"),
        P(),
        P(),
        P(),
        P(),
    )
    return jax.shard_map(
        on_device, mesh=mesh, in_specs=placed, out_specs=P("head", "seq"), check_vma=False
    )
```

time: 353 us -> 248 us (0.70)
  waiting for transfers between devices: 254 us -> 76.3 us
  starting transfers between devices: 4.66 us -> 62.3 us
  Pallas kernels: 52.4 us -> 60.4 us
  local copies, waits for them, and re-layouts: 11.6 us -> 19.1 us
  other arithmetic: 7.53 us -> 13.8 us
  matrix products: 5.86 us -> 0 us
    all_gather x2 -> x0, waiting for transfers between devices: 144 us -> none  [the longest x1 90.6 us: on_device(): key_values = lax.all_gather(slot_kv, 'seq', axis=0)]
    reduce_scatter x1 -> x0, waiting for transfers between devices: 84.5 us -> none  [on_device(): lax.psum_scatter(partial_value, 'head', scatter_dimension=1, tiled=True)]
    ppermute x0 -> x34, waiting for transfers between devices: none -> 76.3 us  [the longest x20 43.5 us: send_seq(): return lax.ppermute(array, 'seq', pairs)]
    ppermute x0 -> x34, starting transfers between devices: none -> 62.3 us  [the longest x20 40.5 us: send_seq(): return lax.ppermute(array, 'seq', pairs)]
    all_to_all x1 -> x0, waiting for transfers between devices: 25.8 us -> none  [sum_at_owner(): lax.all_to_all(blocks, axis, split_axis=0, concat_axis=0, tiled=True)]
    pallas_call x1 -> x5, Pallas kernels: 52.4 us -> 60.4 us  [the longest x1 30.7 us: on_device(): pl.pallas_call(functools.partial(held_kernel, head_size), in_specs=[smem]...]
    another operation x1 -> x6, local copies, waits for them, and re-layouts: 3.56 us -> 10.3 us  [the longest x2 7.63 us: on_device(): ids = jnp.stack(held_ids + once_ids * 2 + twice_ids * 2).astype(jnp.int32)]
    dot_general x1 -> x0, matrix products: 5.86 us -> none  [on_device(): jnp.dot(lax.all_gather(cross_context, 'seq', axis=0, tiled=True), out_wei...]
  transfers between devices with their start and end apart: 4 -> 34, of which waited for: 4 -> 17; matrix products, arithmetic and copies ran while one was open for 0% -> 10% of each run, Pallas kernels for 0% -> 13%
where the time goes in v2:
time: 248 us; the launch traced here: 244 us
  waiting for transfers between devices  76.3 us (31%)
  starting transfers between devices  62.3 us (25%)
  Pallas kernels  60.4 us (24%)
  local copies, waits for them, and re-layouts  19.1 us (8%)
  other arithmetic  13.8 us (6%)
  between operations  11.9 us (5%)
    ppermute x20, waiting for transfers between devices, send_seq(): return lax.ppermute(array, 'seq', pairs)  43.5 us
    ppermute x20, starting transfers between devices, send_seq(): return lax.ppermute(array, 'seq', pairs)  40.5 us
    ppermute x14, waiting for transfers between devices, send_head(): lax.ppermute(array, 'head', [(head_at(a, b), head_at(a + x, b + z)) for a...  32.8 us
    pallas_call x1, Pallas kernels, on_device(): pl.pallas_call(functools.partial(held_kernel, head_size), in_specs=[smem]...  30.7 us
    ppermute x14, starting transfers between devices, send_head(): lax.ppermute(array, 'head', [(head_at(a, b), head_at(a + x, b + z)) for a...  21.9 us
    pallas_call x1, Pallas kernels, on_device(): pl.pallas_call(functools.partial(rebuilt_kernel, head_size), in_specs=[sm...  14.6 us
    another operation x2, local copies, waits for them, and re-layouts, on_device(): ids = jnp.stack(held_ids + once_ids * 2 + twice_ids * 2).astype(jnp.int32)  7.63 us
    pallas_call x1, Pallas kernels, rebuild_parts(): pl.pallas_call(rebuild_kernel, grid_spec=pltpu.PrefetchScalarGridSpec(num...  7.23 us
  transfers between devices with their start and end apart: 34, of which 17 were waited for; matrix products, arithmetic and copies ran while one was open for 10% of the time, Pallas kernels for 13%

profile of v2, /device:TPU:0, one launch (start us, length us, event | category | flops | bytes accessed | tf_op | source)
XLA Modules:
  0.0 243.8 jit_solution(7632066094433900613)
XLA Ops:
  0.0 1.6 dynamic-slice_bitcast_fusion
  3.6 1.6 collective-permute-done.15
  5.2 4.1 %broadcast_select_fusion.1 = (bf16[800,1024]{1,0:T(8,128)(2,1)S(1)}, bf16[800,1024]{1,0:T(8,128)(2,1)}) fusion(bf16[800,1024]{1,0:T(8,128)(2,1)S(1)} %collective-permute-done.15, pred[]{:T(512)} %eq.142, bf16[1,1600,1024]{2,1,0:T(8,128)(2,1)} %param.16, s32[]{:T(128)S(6)} %select_n.423), kind=kLoop, calls=%fused_computation.13 | loop fusion | flops 819200 | bytes 6553605 | tf_op jit(solution)/shard_map/jit(_where)/select_n | solution.py:366
  9.3 7.2 %rebuild_parts.3 = (bf16[800,256]{1,0:T(8,128)(2,1)S(1)}, bf16[800,256]{1,0:T(8,128)(2,1)S(1)}, bf16[800,256]{1,0:T(8,128)(2,1)S(1)}, bf16[800,256]{1,0:T(8,128)...) custom-call(s32[8]{0:T(128)S(1)} %stack.170.order_ref, ...), custom_call_target="tpu_custom_call" | custom-call | tf_op jit(solution)/shard_map/rebuild_parts/pallas_call | solution.py:78
  18.1 1.6 collective-permute-start.20
  21.0 1.9 conditional.1
  23.0 3.2 %collective-permute-start.10 = (bf16[128,1024]{1,0:T(8,128)(2,1)S(1)}, bf16[128,1024]{1,0:T(8,128)(2,1)S(1)}, u32[]{:S(2)}, u32[]{:S(2)}) collective-permute-start(bf16[128,1024]{1,0:T(8,128)(2,1)S(1)} %copy-done.2), channel_id=1, source_target_pairs={{0,64},{8,72},{16,80},{24,88},{32,96},{40,104},{48,112},{56,120},{... | collective-permute-start | bytes 786440 | tf_op jit(solution)/shard_map/ppermute | solution.py:29
  26.2 2.7 %collective-permute-start.13 = (bf16[1600,256]{1,0:T(8,128)(2,1)S(1)}, bf16[1600,256]{1,0:T(8,128)(2,1)}, u32[]{:S(2)}, u32[]{:S(2)}) collective-permute-start(bf16[1600,256]{1,0:T(8,128)(2,1)S(1)} %bitcast.83), channel_id=1, source_target_pairs={{0,16},{8,24},{16,0},{24,8},{32,48},{40,56},{48,32},{56,40},{64,80... | collective-permute-start | bytes 2457608 | tf_op jit(solution)/shard_map/ppermute | solution.py:29
  29.0 4.1 %collective-permute-start.17 = (bf16[800,256]{1,0:T(8,128)(2,1)}, bf16[800,256]{1,0:T(8,128)(2,1)S(1)}, u32[]{:S(2)}, u32[]{:S(2)}) collective-permute-start(bf16[800,256]{1,0:T(8,128)(2,1)} %copy-done.4), channel_id=1, source_target_pairs={{0,3},{1,0},{2,1},{3,2},{4,7},{5,4},{6,5},{7,6},{8,11},{9,8},{10,9... | collective-permute-start | bytes 1228808 | tf_op jit(solution)/shard_map/ppermute | solution.py:33
  34.5 7.1 %collective-permute-done.17 = bf16[800,256]{1,0:T(8,128)(2,1)S(1)} collective-permute-done((bf16[800,256]{1,0:T(8,128)(2,1)}, bf16[800,256]{1,0:T(8,128)(2,1)S(1)}, u32[]{:S(2)}, u32[]{:S(2)}) %collective-permute-start.17) | collective-permute-done | bytes 409632 | tf_op jit(solution)/shard_map/ppermute | solution.py:33
  41.6 3.6 %collective-permute-start.16 = (bf16[800,256]{1,0:T(8,128)(2,1)S(1)}, bf16[800,256]{1,0:T(8,128)(2,1)S(1)}, u32[]{:S(2)}, u32[]{:S(2)}) collective-permute-start(bf16[800,256]{1,0:T(8,128)(2,1)S(1)} %get-tuple-element.62), channel_id=1, source_target_pairs={{0,3},{1,0},{2,1},{3,2},{4,7},{5,4},{6,5},{7,6},{8,11},{9,8},{10,9... | collective-permute-start | bytes 1228808 | tf_op jit(solution)/shard_map/ppermute | solution.py:33
  46.0 10.2 %collective-permute-done.19 = bf16[800,256]{1,0:T(8,128)(2,1)S(1)} collective-permute-done((bf16[800,256]{1,0:T(8,128)(2,1)}, bf16[800,256]{1,0:T(8,128)(2,1)S(1)}, u32[]{:S(2)}, u32[]{:S(2)}) %collective-permute-start.19) | collective-permute-done | bytes 409632 | tf_op jit(solution)/shard_map/ppermute | solution.py:33
  56.2 1.6 collective-permute-start.18
  58.7 2.1 collective-permute-start.22
  72.0 2.4 stack.160
  74.4 5.1 %stack.153 = s32[12]{0:T(128)S(1)} concatenate(s32[1]{0:T(128)} %bitcast.21, s32[1]{0:T(128)} %bitcast.22, s32[1]{0:T(128)} %bitcast.23, s32[1]{0:T(128)} %bitcast.24, s32[1]{0:T(128)} %bitcast.16, s32[1]{0:T(128)} %bitcast.17, s32[1]{0:T(128)} %bitcast.16, s32[1]{0:T(128)} %bitcast.17, s32[1]{0:T(128)} %bitcast.18, s32[1]{0:T(128)} %bitcast.19, s32[1]{0:T(128)} %bitcast.18, ...), dimensions={0} | concatenate | bytes 96 | tf_op jit(solution)/shard_map/stack | solution.py:327
  79.9 3.1 %collective-permute-start.9 = (bf16[128,1024]{1,0:T(8,128)(2,1)S(1)}, bf16[128,1024]{1,0:T(8,128)(2,1)}, u32[]{:S(2)}, u32[]{:S(2)}) collective-permute-start(bf16[128,1024]{1,0:T(8,128)(2,1)S(1)} %copy-done.2), channel_id=1, source_target_pairs={{0,96},{8,104},{16,112},{24,120},{32,0},{40,8},{48,16},{56,24},{64... | collective-permute-start | bytes 786440 | tf_op jit(solution)/shard_map/ppermute | solution.py:29
  84.2 2.8 %collective-permute-start.23 = (bf16[800,256]{1,0:T(8,128)(2,1)S(1)}, bf16[800,256]{1,0:T(8,128)(2,1)S(1)}, u32[]{:S(2)}, u32[]{:S(2)}) collective-permute-start(bf16[800,256]{1,0:T(8,128)(2,1)S(1)} %pad_maximum_fusion.3), channel_id=1, source_target_pairs={{0,16},{8,24},{16,0},{24,8},{32,48},{40,56},{48,32},{56,40},{64,80... | collective-permute-start | bytes 1228808 | tf_op jit(solution)/shard_map/ppermute | solution.py:29
  87.2 10.0 %collective-permute-done.23 = bf16[800,256]{1,0:T(8,128)(2,1)S(1)} collective-permute-done((bf16[800,256]{1,0:T(8,128)(2,1)S(1)}, bf16[800,256]{1,0:T(8,128)(2,1)S(1)}, u32[]{:S(2)}, u32[]{:S(2)}) %collective-permute-start.23) | collective-permute-done | bytes 409632 | tf_op jit(solution)/shard_map/ppermute | solution.py:29
  98.1 2.6 %pad_add_fusion.1.ids = s32[4]{0:T(128)S(1)} fusion(s32[1]{0:T(128)} %bitcast.24, s32[1]{0:T(128)} %bitcast.23, s32[1]{0:T(128)} %bitcast.22, s32[1]{0:T(128)} %bitcast.21), kind=kLoop, calls=%fused_computation.70 | loop fusion | flops 12 | bytes 32 | tf_op jit(solution)/shard_map/stack | solution.py:327
  100.7 2.6 %stack.151.ids = s32[8]{0:T(128)S(1)} concatenate(s32[1]{0:T(128)} %bitcast.16, s32[1]{0:T(128)} %bitcast.17, s32[1]{0:T(128)} %bitcast.16, s32[1]{0:T(128)} %bitcast.17, s32[1]{0:T(128)} %bitcast.18, s32[1]{0:T(128)} %bitcast.19, s32[1]{0:T(128)} %bitcast.18, s32[1]{0:T(128)} %bitcast.19), dimensions={0} | concatenate | bytes 64 | tf_op jit(solution)/shard_map/stack | solution.py:327
  103.9 4.3 %collective-permute-done.11.q3 = bf16[128,1024]{1,0:T(8,128)(2,1)} collective-permute-done((bf16[128,1024]{1,0:T(8,128)(2,1)S(1)}, bf16[128,1024]{1,0:T(8,128)(2,1)}, u32[]{:S(2)}, u32[]{:S(2)}) %collective-permute-start.11) | collective-permute-done | bytes 262176 | tf_op jit(solution)/shard_map/ppermute | solution.py:29
  108.1 30.7 %attend_held.1 = (bf16[16,256,128]{2,1,0:T(8,128)(2,1)S(1)}, f32[16,256,1]{2,1,0:T(8,128)}, f32[16,256,1]{2,1,0:T(8,128)}, f32[16,256,128]{2,1,0:T(8,128)}) custom-call(s32[4]{0:T(128)S(1)} %pad_add_fusion.1.ids, s32[4]{0:T(128)S(1)} %bitcast.86, s32[72]{0:T(128)S(1)} %reshape.168.lists, bf16[128,1024]{1,0:T(8,128)(2,1)S(1)} %copy-done.2, ...), custom_call_target="tpu_custom_call" | custom-call | tf_op jit(solution)/shard_map/attend_held/pallas_call | solution.py:354
  138.8 14.6 %attend_rebuilt.1 = (bf16[128,1152]{1,0:T(8,128)(2,1)S(1)}, bf16[128,1152]{1,0:T(8,128)(2,1)S(1)}, bf16[128,1152]{1,0:T(8,128)(2,1)S(1)}, bf16[128,1152]{1,0:T(8,128)(2,1)S(1)}) custom-call(s32[8]{0:T(128)S(1)} %stack.151.ids, s32[8]{0:T(128)S(1)} %slice.44.count, s32[144]{0:T(256)S(1)} %reshape.167.lists, bf16[16,256,128]{2,1,0:T(8,128)(2,1)S(1)} %get-tuple-element.57.qs, ...), custom_call_target="tpu_custom_call" | custom-call | tf_op jit(solution)/shard_map/attend_rebuilt/pallas_call | solution.py:373
  153.4 9.0 %collective-permute-start.25 = (bf16[128,1152]{1,0:T(8,128)(2,1)S(1)}, bf16[128,1152]{1,0:T(8,128)(2,1)S(1)}, u32[]{:S(2)}, u32[]{:S(2)}) collective-permute-start(bf16[128,1152]{1,0:T(8,128)(2,1)S(1)} %get-tuple-element.72), channel_id=1, source_target_pairs={{0,32},{8,40},{16,48},{24,56},{32,64},{40,72},{48,80},{56,88},{64,... | collective-permute-start | bytes 884744 | tf_op jit(solution)/shard_map/ppermute | solution.py:29
  162.4 2.8 %collective-permute-start.27 = (bf16[128,1152]{1,0:T(8,128)(2,1)S(1)}, bf16[128,1152]{1,0:T(8,128)(2,1)S(1)}, u32[]{:S(2)}, u32[]{:S(2)}) collective-permute-start(bf16[128,1152]{1,0:T(8,128)(2,1)S(1)} %get-tuple-element.74), channel_id=1, source_target_pairs={{0,96},{8,104},{16,112},{24,120},{32,0},{40,8},{48,16},{56,24},{64... | collective-permute-start | bytes 884744 | tf_op jit(solution)/shard_map/ppermute | solution.py:29
  165.1 2.8 %collective-permute-done.25.b = bf16[128,1152]{1,0:T(8,128)(2,1)S(1)} collective-permute-done((bf16[128,1152]{1,0:T(8,128)(2,1)S(1)}, bf16[128,1152]{1,0:T(8,128)(2,1)S(1)}, u32[]{:S(2)}, u32[]{:S(2)}) %collective-permute-start.25) | collective-permute-done | bytes 294944 | tf_op jit(solution)/shard_map/ppermute | solution.py:29
  167.9 6.3 %collective-permute-done.26.c = bf16[128,1152]{1,0:T(8,128)(2,1)S(1)} collective-permute-done((bf16[128,1152]{1,0:T(8,128)(2,1)S(1)}, bf16[128,1152]{1,0:T(8,128)(2,1)S(1)}, u32[]{:S(2)}, u32[]{:S(2)}) %collective-permute-start.26) | collective-permute-done | bytes 294944 | tf_op jit(solution)/shard_map/ppermute | solution.py:29
  174.3 1.1 collective-permute-done.27.d
  176.3 4.7 %collective-permute-start.31 = (bf16[128,1024]{1,0:T(8,128)(2,1)S(1)}, bf16[128,1024]{1,0:T(8,128)(2,1)S(1)}, u32[]{:S(2)}, u32[]{:S(2)}) collective-permute-start(bf16[128,1024]{1,0:T(8,128)(2,1)S(1)} %merge.1), channel_id=1, source_target_pairs={{0,32},{8,40},{16,48},{24,56},{32,64},{40,72},{48,80},{56,88},{64,... | collective-permute-start | bytes 786440 | tf_op jit(solution)/shard_map/ppermute | solution.py:29
  181.0 3.0 %collective-permute-start.28 = (bf16[128,1024]{1,0:T(8,128)(2,1)S(1)}, bf16[128,1024]{1,0:T(8,128)(2,1)S(1)}, u32[]{:S(2)}, u32[]{:S(2)}) collective-permute-start(bf16[128,1024]{1,0:T(8,128)(2,1)S(1)} %merge.1), channel_id=1, source_target_pairs={{0,16},{8,24},{16,0},{24,8},{32,48},{40,56},{48,32},{56,40},{64,80... | collective-permute-start | bytes 786440 | tf_op jit(solution)/shard_map/ppermute | solution.py:29
  184.5 2.6 %collective-permute-done.31 = bf16[128,1024]{1,0:T(8,128)(2,1)S(1)} collective-permute-done((bf16[128,1024]{1,0:T(8,128)(2,1)S(1)}, bf16[128,1024]{1,0:T(8,128)(2,1)S(1)}, u32[]{:S(2)}, u32[]{:S(2)}) %collective-permute-start.31) | collective-permute-done | bytes 262176 | tf_op jit(solution)/shard_map/ppermute | solution.py:29
  187.1 3.3 %collective-permute-start.34 = (bf16[128,1024]{1,0:T(8,128)(2,1)S(1)}, bf16[128,1024]{1,0:T(8,128)(2,1)S(1)}, u32[]{:S(2)}, u32[]{:S(2)}) collective-permute-start(bf16[128,1024]{1,0:T(8,128)(2,1)S(1)} %collective-permute-done.31), channel_id=1, source_target_pairs={{0,16},{8,24},{16,0},{24,8},{32,48},{40,56},{48,32},{56,40},{64,80... | collective-permute-start | bytes 786440 | tf_op jit(solution)/shard_map/ppermute | solution.py:29
  190.4 1.4 collective-permute-start.32
  191.8 1.8 collective-permute-start.30
  193.7 4.6 %collective-permute-done.32 = bf16[128,1024]{1,0:T(8,128)(2,1)S(1)} collective-permute-done((bf16[128,1024]{1,0:T(8,128)(2,1)S(1)}, bf16[128,1024]{1,0:T(8,128)(2,1)S(1)}, u32[]{:S(2)}, u32[]{:S(2)}) %collective-permute-start.32) | collective-permute-done | bytes 262176 | tf_op jit(solution)/shard_map/ppermute | solution.py:29
  198.3 1.3 collective-permute-start.33
  199.7 6.5 %collective-permute-done.33 = bf16[128,1024]{1,0:T(8,128)(2,1)S(1)} collective-permute-done((bf16[128,1024]{1,0:T(8,128)(2,1)S(1)}, bf16[128,1024]{1,0:T(8,128)(2,1)S(1)}, u32[]{:S(2)}, u32[]{:S(2)}) %collective-permute-start.33) | collective-permute-done | bytes 262176 | tf_op jit(solution)/shard_map/ppermute | solution.py:29
  207.0 3.6 %collective-permute-done.35.other_ref = bf16[8,128,1024]{2,1,0:T(8,128)(2,1)} collective-permute-done((bf16[8,128,1024]{2,1,0:T(8,128)(2,1)S(1)}, bf16[8,128,1024]{2,1,0:T(8,128)(2,1)}, u32[]{:S(2)}, u32[]{:S(2)}) %collective-permute-start.35) | collective-permute-done | bytes 2097184 | tf_op jit(solution)/shard_map/ppermute | solution.py:29
  210.6 7.0 %project_parts.1 = (bf16[256,512]{1,0:T(8,128)(2,1)S(1)}, bf16[256,512]{1,0:T(8,128)(2,1)S(1)}, bf16[256,512]{1,0:T(8,128)(2,1)S(1)}, bf16[256,512]{1,0:T(8,128)...) custom-call(s32[8]{0:T(128)S(1)} %stack.148.order_ref, ...), custom_call_target="tpu_custom_call" | custom-call | tf_op jit(solution)/shard_map/project_parts/pallas_call | solution.py:112
  217.9 2.1 collective-permute-start.37
  220.1 1.8 collective-permute-start.39
  221.9 5.0 %collective-permute-done.40 = bf16[256,512]{1,0:T(8,128)(2,1)S(1)} collective-permute-done((bf16[256,512]{1,0:T(8,128)(2,1)S(1)}, bf16[256,512]{1,0:T(8,128)(2,1)S(1)}, u32[]{:S(2)}, u32[]{:S(2)}) %collective-permute-start.40) | collective-permute-done | bytes 262176 | tf_op jit(solution)/shard_map/ppermute | solution.py:33
  226.9 2.0 collective-permute-start.41
  228.9 1.3 collective-permute-start.36
  230.6 1.8 collective-permute-done.39
  232.4 2.6 %collective-permute-done.41 = bf16[256,512]{1,0:T(8,128)(2,1)S(1)} collective-permute-done((bf16[256,512]{1,0:T(8,128)(2,1)S(1)}, bf16[256,512]{1,0:T(8,128)(2,1)S(1)}, u32[]{:S(2)}, u32[]{:S(2)}) %collective-permute-start.41) | collective-permute-done | bytes 262176 | tf_op jit(solution)/shard_map/ppermute | solution.py:33
  237.3 5.4 %collective-permute-done.42 = bf16[256,512]{1,0:T(8,128)(2,1)S(1)} collective-permute-done((bf16[256,512]{1,0:T(8,128)(2,1)S(1)}, bf16[256,512]{1,0:T(8,128)(2,1)S(1)}, u32[]{:S(2)}, u32[]{:S(2)}) %collective-permute-start.42) | collective-permute-done | bytes 262176 | tf_op jit(solution)/shard_map/ppermute | solution.py:33
  (114 shorter events, 19.2 us)
Async XLA Ops:
  0.0 1.9 copy-start.11
  0.0 2.1 copy-start.12
  1.6 3.6 %collective-permute-start.15 = (bf16[800,1024]{1,0:T(8,128)(2,1)S(1)}, bf16[800,1024]{1,0:T(8,128)(2,1)S(1)}, u32[]{:S(2)}, u32[]{:S(2)}) collective-permute-start(bf16[800,1024]{1,0:T(8,128)(2,1)S(1)} %dynamic-slice_bitcast_fusion), channel_id=1, source_target_pairs={{0,8},{8,0},{16,24},{24,16},{32,40},{40,32},{48,56},{56,48},{64,72... | collective-permute-start | bytes 4915208 | tf_op jit(solution)/shard_map/ppermute | solution.py:29
  3.6 5.7 %copy-start.5 = (bf16[1024,2048]{1,0:T(8,128)(2,1)S(1)}, bf16[1024,2048]{1,0:T(8,128)(2,1)}, u32[]{:S(2)}) copy-start(bf16[1024,2048]{1,0:T(8,128)(2,1)} %proj_ref.1) | copy-start | bytes 12582916
  5.2 4.1 %copy-start.7 = (bf16[800,1024]{1,0:T(8,128)(2,1)}, bf16[800,1024]{1,0:T(8,128)(2,1)S(1)}, u32[]{:S(2)}) copy-start(bf16[800,1024]{1,0:T(8,128)(2,1)S(1)} %collective-permute-done.15) | copy-start | bytes 4915204
  9.3 11.7 %copy-start.10 = (f32[128]{0:T(128)S(1)}, f32[128]{0:T(128)}, u32[]{:S(2)}) copy-start(f32[128]{0:T(128)} %param.18) | copy-start | bytes 1540
  16.5 0.8 copy-start.3
  17.3 0.8 copy-start.4
  18.1 15.2 %collective-permute-start.20 = (bf16[800,256]{1,0:T(8,128)(2,1)}, bf16[800,256]{1,0:T(8,128)(2,1)}, u32[]{:S(2)}, u32[]{:S(2)}) collective-permute-start(bf16[800,256]{1,0:T(8,128)(2,1)} %get-tuple-element.68), channel_id=1, source_target_pairs={{0,4},{1,5},{2,6},{3,7},{4,0},{5,1},{6,2},{7,3},{8,12},{9,13},{10,... | collective-permute-start | bytes 1228808 | tf_op jit(solution)/shard_map/ppermute | solution.py:33
  21.0 2.0 copy-start.2
  21.0 5.2 %copy-start.1 = (bf16[1,1600,256]{2,1,0:T(8,128)(2,1)S(1)}, bf16[1,1600,256]{2,1,0:T(8,128)(2,1)}, u32[]{:S(2)}) copy-start(bf16[1,1600,256]{2,1,0:T(8,128)(2,1)} %param.15) | copy-start | bytes 2457604
  21.0 7.9 %copy-start.9 = (s32[2048,2]{0,1:T(2,128)S(1)}, s32[2048,2]{0,1:T(2,128)}, u32[]{:S(2)}) copy-start(s32[2048,2]{0,1:T(2,128)} %param.21) | copy-start | bytes 49156
  23.0 75.0 %collective-permute-start.10 = (bf16[128,1024]{1,0:T(8,128)(2,1)S(1)}, bf16[128,1024]{1,0:T(8,128)(2,1)S(1)}, u32[]{:S(2)}, u32[]{:S(2)}) collective-permute-start(bf16[128,1024]{1,0:T(8,128)(2,1)S(1)} %copy-done.2), channel_id=1, source_target_pairs={{0,64},{8,72},{16,80},{24,88},{32,96},{40,104},{48,112},{56,120},{... | collective-permute-start | bytes 786440 | tf_op jit(solution)/shard_map/ppermute | solution.py:29
  26.2 53.7 %collective-permute-start.13 = (bf16[1600,256]{1,0:T(8,128)(2,1)S(1)}, bf16[1600,256]{1,0:T(8,128)(2,1)}, u32[]{:S(2)}, u32[]{:S(2)}) collective-permute-start(bf16[1600,256]{1,0:T(8,128)(2,1)S(1)} %bitcast.83), channel_id=1, source_target_pairs={{0,16},{8,24},{16,0},{24,8},{32,48},{40,56},{48,32},{56,40},{64,80... | collective-permute-start | bytes 2457608 | tf_op jit(solution)/shard_map/ppermute | solution.py:29
  29.0 12.6 %collective-permute-start.17 = (bf16[800,256]{1,0:T(8,128)(2,1)}, bf16[800,256]{1,0:T(8,128)(2,1)S(1)}, u32[]{:S(2)}, u32[]{:S(2)}) collective-permute-start(bf16[800,256]{1,0:T(8,128)(2,1)} %copy-done.4), channel_id=1, source_target_pairs={{0,3},{1,0},{2,1},{3,2},{4,7},{5,4},{6,5},{7,6},{8,11},{9,8},{10,9... | collective-permute-start | bytes 1228808 | tf_op jit(solution)/shard_map/ppermute | solution.py:33
  33.1 23.1 %collective-permute-start.19 = (bf16[800,256]{1,0:T(8,128)(2,1)}, bf16[800,256]{1,0:T(8,128)(2,1)S(1)}, u32[]{:S(2)}, u32[]{:S(2)}) collective-permute-start(bf16[800,256]{1,0:T(8,128)(2,1)} %copy-done.3), channel_id=1, source_target_pairs={{0,4},{1,5},{2,6},{3,7},{4,0},{5,1},{6,2},{7,3},{8,12},{9,13},{10,... | collective-permute-start | bytes 1228808 | tf_op jit(solution)/shard_map/ppermute | solution.py:33
  34.4 23.4 %collective-permute-start.21 = (bf16[800,256]{1,0:T(8,128)(2,1)S(1)}, bf16[800,256]{1,0:T(8,128)(2,1)S(1)}, u32[]{:S(2)}, u32[]{:S(2)}) collective-permute-start(bf16[800,256]{1,0:T(8,128)(2,1)S(1)} %add_convert_fusion.4), channel_id=1, source_target_pairs={{0,1},{1,2},{2,3},{3,0},{4,5},{5,6},{6,7},{7,4},{8,9},{9,10},{10,1... | collective-permute-start | bytes 1228808 | tf_op jit(solution)/shard_map/ppermute | solution.py:33
  41.6 41.4 %collective-permute-start.16 = (bf16[800,256]{1,0:T(8,128)(2,1)S(1)}, bf16[800,256]{1,0:T(8,128)(2,1)S(1)}, u32[]{:S(2)}, u32[]{:S(2)}) collective-permute-start(bf16[800,256]{1,0:T(8,128)(2,1)S(1)} %get-tuple-element.62), channel_id=1, source_target_pairs={{0,3},{1,0},{2,1},{3,2},{4,7},{5,4},{6,5},{7,6},{8,11},{9,8},{10,9... | collective-permute-start | bytes 1228808 | tf_op jit(solution)/shard_map/ppermute | solution.py:33
  56.2 26.8 %collective-permute-start.18 = (bf16[800,256]{1,0:T(8,128)(2,1)}, bf16[800,256]{1,0:T(8,128)(2,1)S(1)}, u32[]{:S(2)}, u32[]{:S(2)}) collective-permute-start(bf16[800,256]{1,0:T(8,128)(2,1)} %add_convert_fusion.5), channel_id=1, source_target_pairs={{0,4},{1,5},{2,6},{3,7},{4,0},{5,1},{6,2},{7,3},{8,12},{9,13},{10,... | collective-permute-start | bytes 1228808 | tf_op jit(solution)/shard_map/ppermute | solution.py:33
  58.7 24.8 %collective-permute-start.22 = (bf16[800,256]{1,0:T(8,128)(2,1)}, bf16[800,256]{1,0:T(8,128)(2,1)S(1)}, u32[]{:S(2)}, u32[]{:S(2)}) collective-permute-start(bf16[800,256]{1,0:T(8,128)(2,1)} %add_convert_fusion.3), channel_id=1, source_target_pairs={{0,1},{1,2},{2,3},{3,0},{4,5},{5,6},{6,7},{7,4},{8,9},{9,10},{10,1... | collective-permute-start | bytes 1228808 | tf_op jit(solution)/shard_map/ppermute | solution.py:33
  79.9 24.0 %collective-permute-start.9 = (bf16[128,1024]{1,0:T(8,128)(2,1)S(1)}, bf16[128,1024]{1,0:T(8,128)(2,1)}, u32[]{:S(2)}, u32[]{:S(2)}) collective-permute-start(bf16[128,1024]{1,0:T(8,128)(2,1)S(1)} %copy-done.2), channel_id=1, source_target_pairs={{0,96},{8,104},{16,112},{24,120},{32,0},{40,8},{48,16},{56,24},{64... | collective-permute-start | bytes 786440 | tf_op jit(solution)/shard_map/ppermute | solution.py:29
  83.0 25.1 %collective-permute-start.12 = (bf16[1600,256]{1,0:T(8,128)(2,1)S(1)}, bf16[1600,256]{1,0:T(8,128)(2,1)}, u32[]{:S(2)}, u32[]{:S(2)}) collective-permute-start(bf16[1600,256]{1,0:T(8,128)(2,1)S(1)} %bitcast.84), channel_id=1, source_target_pairs={{0,8},{8,0},{16,24},{24,16},{32,40},{40,32},{48,56},{56,48},{64,72... | collective-permute-start | bytes 2457608 | tf_op jit(solution)/shard_map/ppermute | solution.py:29
  83.0 25.1 %collective-permute-start.14 = (bf16[1600,256]{1,0:T(8,128)(2,1)}, bf16[1600,256]{1,0:T(8,128)(2,1)}, u32[]{:S(2)}, u32[]{:S(2)}) collective-permute-start(bf16[1600,256]{1,0:T(8,128)(2,1)} %collective-permute-done.13.c), channel_id=1, source_target_pairs={{0,8},{8,0},{16,24},{24,16},{32,40},{40,32},{48,56},{56,48},{64,72... | collective-permute-start | bytes 2457608 | tf_op jit(solution)/shard_map/ppermute | solution.py:29
  84.2 13.0 %collective-permute-start.23 = (bf16[800,256]{1,0:T(8,128)(2,1)S(1)}, bf16[800,256]{1,0:T(8,128)(2,1)S(1)}, u32[]{:S(2)}, u32[]{:S(2)}) collective-permute-start(bf16[800,256]{1,0:T(8,128)(2,1)S(1)} %pad_maximum_fusion.3), channel_id=1, source_target_pairs={{0,16},{8,24},{16,0},{24,8},{32,48},{40,56},{48,32},{56,40},{64,80... | collective-permute-start | bytes 1228808 | tf_op jit(solution)/shard_map/ppermute | solution.py:29
  97.3 41.5 %collective-permute-start.24 = (bf16[2,800,256]{2,1,0:T(8,128)(2,1)S(1)}, bf16[2,800,256]{2,1,0:T(8,128)(2,1)S(1)}, u32[]{:S(2)}, u32[]{:S(2)}) collective-permute-start(bf16[2,800,256]{2,1,0:T(8,128)(2,1)S(1)} %pad_maximum_fusion.2.a), channel_id=1, source_target_pairs={{0,8},{8,0},{16,24},{24,16},{32,40},{40,32},{48,56},{56,48},{64,72... | collective-permute-start | bytes 2457608 | tf_op jit(solution)/shard_map/ppermute | solution.py:29
  98.0 10.1 %collective-permute-start.11 = (bf16[128,1024]{1,0:T(8,128)(2,1)S(1)}, bf16[128,1024]{1,0:T(8,128)(2,1)}, u32[]{:S(2)}, u32[]{:S(2)}) collective-permute-start(bf16[128,1024]{1,0:T(8,128)(2,1)S(1)} %copy-done.2), channel_id=1, source_target_pairs={{0,32},{8,40},{16,48},{24,56},{32,64},{40,72},{48,80},{56,88},{64,... | collective-permute-start | bytes 786440 | tf_op jit(solution)/shard_map/ppermute | solution.py:29
  153.4 14.6 %collective-permute-start.25 = (bf16[128,1152]{1,0:T(8,128)(2,1)S(1)}, bf16[128,1152]{1,0:T(8,128)(2,1)S(1)}, u32[]{:S(2)}, u32[]{:S(2)}) collective-permute-start(bf16[128,1152]{1,0:T(8,128)(2,1)S(1)} %get-tuple-element.72), channel_id=1, source_target_pairs={{0,32},{8,40},{16,48},{24,56},{32,64},{40,72},{48,80},{56,88},{64,... | collective-permute-start | bytes 884744 | tf_op jit(solution)/shard_map/ppermute | solution.py:29
  162.4 11.9 %collective-permute-start.26 = (bf16[128,1152]{1,0:T(8,128)(2,1)S(1)}, bf16[128,1152]{1,0:T(8,128)(2,1)S(1)}, u32[]{:S(2)}, u32[]{:S(2)}) collective-permute-start(bf16[128,1152]{1,0:T(8,128)(2,1)S(1)} %get-tuple-element.73), channel_id=1, source_target_pairs={{0,64},{8,72},{16,80},{24,88},{32,96},{40,104},{48,112},{56,120},{... | collective-permute-start | bytes 884744 | tf_op jit(solution)/shard_map/ppermute | solution.py:29
  162.4 13.0 %collective-permute-start.27 = (bf16[128,1152]{1,0:T(8,128)(2,1)S(1)}, bf16[128,1152]{1,0:T(8,128)(2,1)S(1)}, u32[]{:S(2)}, u32[]{:S(2)}) collective-permute-start(bf16[128,1152]{1,0:T(8,128)(2,1)S(1)} %get-tuple-element.74), channel_id=1, source_target_pairs={{0,96},{8,104},{16,112},{24,120},{32,0},{40,8},{48,16},{56,24},{64... | collective-permute-start | bytes 884744 | tf_op jit(solution)/shard_map/ppermute | solution.py:29
  176.3 10.8 %collective-permute-start.31 = (bf16[128,1024]{1,0:T(8,128)(2,1)S(1)}, bf16[128,1024]{1,0:T(8,128)(2,1)S(1)}, u32[]{:S(2)}, u32[]{:S(2)}) collective-permute-start(bf16[128,1024]{1,0:T(8,128)(2,1)S(1)} %merge.1), channel_id=1, source_target_pairs={{0,32},{8,40},{16,48},{24,56},{32,64},{40,72},{48,80},{56,88},{64,... | collective-permute-start | bytes 786440 | tf_op jit(solution)/shard_map/ppermute | solution.py:29
  181.0 10.8 %collective-permute-start.28 = (bf16[128,1024]{1,0:T(8,128)(2,1)S(1)}, bf16[128,1024]{1,0:T(8,128)(2,1)S(1)}, u32[]{:S(2)}, u32[]{:S(2)}) collective-permute-start(bf16[128,1024]{1,0:T(8,128)(2,1)S(1)} %merge.1), channel_id=1, source_target_pairs={{0,16},{8,24},{16,0},{24,8},{32,48},{40,56},{48,32},{56,40},{64,80... | collective-permute-start | bytes 786440 | tf_op jit(solution)/shard_map/ppermute | solution.py:29
  184.0 9.6 %collective-permute-start.29 = (bf16[128,1024]{1,0:T(8,128)(2,1)S(1)}, bf16[128,1024]{1,0:T(8,128)(2,1)S(1)}, u32[]{:S(2)}, u32[]{:S(2)}) collective-permute-start(bf16[128,1024]{1,0:T(8,128)(2,1)S(1)} %merge.1), channel_id=1, source_target_pairs={{0,96},{8,104},{16,112},{24,120},{32,0},{40,8},{48,16},{56,24},{64... | collective-permute-start | bytes 786440 | tf_op jit(solution)/shard_map/ppermute | solution.py:29
  184.5 26.1 %copy-start = (bf16[1024,512]{1,0:T(8,128)(2,1)S(1)}, bf16[1024,512]{1,0:T(8,128)(2,1)}, u32[]{:S(2)}) copy-start(bf16[1024,512]{1,0:T(8,128)(2,1)} %weight_ref.1) | copy-start | bytes 3145732
  187.1 19.2 %collective-permute-start.34 = (bf16[128,1024]{1,0:T(8,128)(2,1)S(1)}, bf16[128,1024]{1,0:T(8,128)(2,1)S(1)}, u32[]{:S(2)}, u32[]{:S(2)}) collective-permute-start(bf16[128,1024]{1,0:T(8,128)(2,1)S(1)} %collective-permute-done.31), channel_id=1, source_target_pairs={{0,16},{8,24},{16,0},{24,8},{32,48},{40,56},{48,32},{56,40},{64,80... | collective-permute-start | bytes 786440 | tf_op jit(solution)/shard_map/ppermute | solution.py:29
  190.4 7.9 %collective-permute-start.32 = (bf16[128,1024]{1,0:T(8,128)(2,1)S(1)}, bf16[128,1024]{1,0:T(8,128)(2,1)S(1)}, u32[]{:S(2)}, u32[]{:S(2)}) collective-permute-start(bf16[128,1024]{1,0:T(8,128)(2,1)S(1)} %collective-permute-done.31), channel_id=1, source_target_pairs={{0,32},{8,40},{16,48},{24,56},{32,64},{40,72},{48,80},{56,88},{64,... | collective-permute-start | bytes 786440 | tf_op jit(solution)/shard_map/ppermute | solution.py:29
  191.8 7.8 %collective-permute-start.30 = (bf16[128,1024]{1,0:T(8,128)(2,1)S(1)}, bf16[128,1024]{1,0:T(8,128)(2,1)S(1)}, u32[]{:S(2)}, u32[]{:S(2)}) collective-permute-start(bf16[128,1024]{1,0:T(8,128)(2,1)S(1)} %collective-permute-done.28), channel_id=1, source_target_pairs={{0,96},{8,104},{16,112},{24,120},{32,0},{40,8},{48,16},{56,24},{64... | collective-permute-start | bytes 786440 | tf_op jit(solution)/shard_map/ppermute | solution.py:29
  198.3 7.9 %collective-permute-start.33 = (bf16[128,1024]{1,0:T(8,128)(2,1)S(1)}, bf16[128,1024]{1,0:T(8,128)(2,1)S(1)}, u32[]{:S(2)}, u32[]{:S(2)}) collective-permute-start(bf16[128,1024]{1,0:T(8,128)(2,1)S(1)} %collective-permute-done.32), channel_id=1, source_target_pairs={{0,16},{8,24},{16,0},{24,8},{32,48},{40,56},{48,32},{56,40},{64,80... | collective-permute-start | bytes 786440 | tf_op jit(solution)/shard_map/ppermute | solution.py:29
  206.3 4.4 %collective-permute-start.35 = (bf16[8,128,1024]{2,1,0:T(8,128)(2,1)S(1)}, bf16[8,128,1024]{2,1,0:T(8,128)(2,1)}, u32[]{:S(2)}, u32[]{:S(2)}) collective-permute-start(bf16[8,128,1024]{2,1,0:T(8,128)(2,1)S(1)} %bitcast_dynamic-update-slice_fusion.own_ref), channel_id=1, source_target_pairs={{0,8},{8,0},{16,24},{24,16},{32,40},{40,32},{48,56},{56,48},{64,72... | collective-permute-start | bytes 6291464 | tf_op jit(solution)/shard_map/ppermute | solution.py:29
  217.6 25.1 %copy-start.8 = (bf16[256,512]{1,0:T(8,128)(2,1)S(1)}, bf16[256,512]{1,0:T(8,128)(2,1)}, u32[]{:S(2)}) copy-start(bf16[256,512]{1,0:T(8,128)(2,1)} %param.13) | copy-start | bytes 786436
  217.6 9.2 %collective-permute-start.40 = (bf16[256,512]{1,0:T(8,128)(2,1)S(1)}, bf16[256,512]{1,0:T(8,128)(2,1)S(1)}, u32[]{:S(2)}, u32[]{:S(2)}) collective-permute-start(bf16[256,512]{1,0:T(8,128)(2,1)S(1)} %get-tuple-element.82), channel_id=1, source_target_pairs={{0,4},{1,5},{2,6},{3,7},{4,0},{5,1},{6,2},{7,3},{8,12},{9,13},{10,... | collective-permute-start | bytes 786440 | tf_op jit(solution)/shard_map/ppermute | solution.py:33
  217.9 12.3 %collective-permute-start.37 = (bf16[256,512]{1,0:T(8,128)(2,1)S(1)}, bf16[256,512]{1,0:T(8,128)(2,1)S(1)}, u32[]{:S(2)}, u32[]{:S(2)}) collective-permute-start(bf16[256,512]{1,0:T(8,128)(2,1)S(1)} %get-tuple-element.78), channel_id=1, source_target_pairs={{0,3},{1,0},{2,1},{3,2},{4,7},{5,4},{6,5},{7,6},{8,11},{9,8},{10,9... | collective-permute-start | bytes 786440 | tf_op jit(solution)/shard_map/ppermute | solution.py:33
  220.1 12.3 %collective-permute-start.39 = (bf16[256,512]{1,0:T(8,128)(2,1)S(1)}, bf16[256,512]{1,0:T(8,128)(2,1)S(1)}, u32[]{:S(2)}, u32[]{:S(2)}) collective-permute-start(bf16[256,512]{1,0:T(8,128)(2,1)S(1)} %get-tuple-element.80), channel_id=1, source_target_pairs={{0,4},{1,5},{2,6},{3,7},{4,0},{5,1},{6,2},{7,3},{8,12},{9,13},{10,... | collective-permute-start | bytes 786440 | tf_op jit(solution)/shard_map/ppermute | solution.py:33
  226.9 8.0 %collective-permute-start.41 = (bf16[256,512]{1,0:T(8,128)(2,1)S(1)}, bf16[256,512]{1,0:T(8,128)(2,1)S(1)}, u32[]{:S(2)}, u32[]{:S(2)}) collective-permute-start(bf16[256,512]{1,0:T(8,128)(2,1)S(1)} %add_convert_fusion.8), channel_id=1, source_target_pairs={{0,1},{1,2},{2,3},{3,0},{4,5},{5,6},{6,7},{7,4},{8,9},{9,10},{10,1... | collective-permute-start | bytes 786440 | tf_op jit(solution)/shard_map/ppermute | solution.py:33
  228.9 7.6 %collective-permute-start.36 = (bf16[256,512]{1,0:T(8,128)(2,1)S(1)}, bf16[256,512]{1,0:T(8,128)(2,1)S(1)}, u32[]{:S(2)}, u32[]{:S(2)}) collective-permute-start(bf16[256,512]{1,0:T(8,128)(2,1)S(1)} %get-tuple-element.76), channel_id=1, source_target_pairs={{0,3},{1,0},{2,1},{3,2},{4,7},{5,4},{6,5},{7,6},{8,11},{9,8},{10,9... | collective-permute-start | bytes 786440 | tf_op jit(solution)/shard_map/ppermute | solution.py:33
  230.3 7.0 %collective-permute-start.38 = (bf16[256,512]{1,0:T(8,128)(2,1)S(1)}, bf16[256,512]{1,0:T(8,128)(2,1)S(1)}, u32[]{:S(2)}, u32[]{:S(2)}) collective-permute-start(bf16[256,512]{1,0:T(8,128)(2,1)S(1)} %add_convert_fusion.9), channel_id=1, source_target_pairs={{0,4},{1,5},{2,6},{3,7},{4,0},{5,1},{6,2},{7,3},{8,12},{9,13},{10,... | collective-permute-start | bytes 786440 | tf_op jit(solution)/shard_map/ppermute | solution.py:33
  235.1 7.7 %collective-permute-start.42 = (bf16[256,512]{1,0:T(8,128)(2,1)S(1)}, bf16[256,512]{1,0:T(8,128)(2,1)S(1)}, u32[]{:S(2)}, u32[]{:S(2)}) collective-permute-start(bf16[256,512]{1,0:T(8,128)(2,1)S(1)} %add_convert_fusion.7), channel_id=1, source_target_pairs={{0,1},{1,2},{2,3},{3,0},{4,5},{5,6},{6,7},{7,4},{8,9},{9,10},{10,1... | collective-permute-start | bytes 786440 | tf_op jit(solution)/shard_map/ppermute | solution.py:33
